TPU v7x, 32 devices: a whole 2x2x4 slice. The times are simulated.
32 devices in a mesh: snode: 8 (over z, x), rhs: 4 (over y, core).
Axes of the slice: x: 2, y: 2, z: 4, core: 2. Of those that a mesh axis runs over, the one named last changes fastest.
Arguments:
- right_sides: float32 [3, 16, 256, 512], P(None, 'snode', None, 'rhs'), may hold values from -6 to 6
- diag_inverse: float32 [3, 16, 256, 256], P(None, 'snode', 'rhs')
- off_diagonal: bfloat16 [2, 16, 1024, 256], P(None, 'snode'), may hold values from -0.125 to 0.125
- target_snode: int32 [2, 16, 64], P(None, 'snode'), may hold values from 0 to 15, as said below
- target_block: int32 [2, 16, 64], P(None, 'snode'), may hold values from 0 to 15
Outputs:
- solution: float32 [3, 16, 256, 512], P(None, 'snode', None, 'rhs')
Inputs may be any that keep to these rules, and one draw needn't show every extreme that they name: `target_snode`: each entry is a supernode's position in the next level; the supernodes at positions i * 2 to i * 2 + 1 belong to index i of snode. Of one level's blocks held by one index of snode, at most 32 name supernodes of any one index, and some index receives exactly 32 from every index in every level.
All inputs are finite; a program needn't handle non-finite values.
Results may differ from a plain program's by a relative error of at most 0.0038.
Values may be sent and summed in bfloat16 or wider, within the bound.
A program may use at most 64 MiB of HBM per device.

v0:
```python
import jax
import jax.numpy as jnp
from jax import lax
from jax.sharding import PartitionSpec as P

BR = 16


def on_device(right_sides, diag_inverse, off_diagonal, target_snode, target_block):
    precise = lax.Precision.HIGHEST
    levels = right_sides.shape[0]
    local_nodes = right_sides.shape[1]
    order_size = right_sides.shape[2]
    columns = right_sides.shape[3]
    per_node = target_snode.shape[2]
    row_blocks = order_size // BR
    devices = lax.axis_size("snode")
    outgoing = local_nodes * per_node
    capacity = 2 * outgoing // devices
    slot_count = devices * capacity
    local_rows = local_nodes * row_blocks
    front_count = 1
    front_width = columns // front_count
    full_diag = [
        lax.all_gather(diag_inverse[height], "rhs", axis=1, tiled=True) for height in range(levels)
    ]
    block_order = lax.iota(jnp.int32, outgoing)
    slot_ids = lax.iota(jnp.int32, slot_count)
    row_ids = lax.iota(jnp.int32, local_rows)
    routes = []
    for height in range(levels - 1):
        flat_target = target_snode[height].reshape(outgoing)
        owner_dev = flat_target // local_nodes
        target_code = flat_target % local_nodes * row_blocks + target_block[height].reshape(
            outgoing
        )
        earlier = (owner_dev[:, None] == owner_dev[None, :]) & (
            block_order[None, :] < block_order[:, None]
        )
        destination = owner_dev * capacity + jnp.sum(earlier.astype(jnp.int32), axis=1)
        placed = destination[None, :] == slot_ids[:, None]
        source = jnp.max(jnp.where(placed, block_order[None, :], -1), axis=1)
        slot_code = jnp.max(jnp.where(placed, target_code[None, :], -1), axis=1).reshape(
            devices, capacity
        )
        routes.append((destination, source, slot_code))
    residual_list = [right_sides[0]]
    lower_sols = [[]]
    arrivals = [[]]
    for height in range(levels):
        front = 0
        solve_result = jnp.einsum(
            "svw,swr->svr", full_diag[height], residual_list[front], precision=precise
        )
        lower_sols[front].append(solve_result)
        if height + 1 < levels:
            destination, source, slot_code = routes[height]
            update = jnp.einsum(
                "skw,swr->skr",
                off_diagonal[height],
                solve_result.astype(jnp.bfloat16),
                preferred_element_type=jnp.float32,
            )
            update = update.astype(jnp.bfloat16).reshape(outgoing, BR * front_width)
            outbound = jnp.where(
                (source >= 0)[:, None], update[jnp.maximum(source, 0)], jnp.zeros((), jnp.bfloat16)
            )
            outbound = outbound.reshape(devices, capacity, BR * front_width)
            inbound, inbound_code = (
                lax.all_to_all(outbound, "snode", split_axis=0, concat_axis=0, tiled=True),
                lax.all_to_all(slot_code, "snode", split_axis=0, concat_axis=0, tiled=True),
            )
            arrived = inbound_code.reshape(slot_count)
            arrivals[front].append(arrived)
            gather_table = (arrived[None, :] == row_ids[:, None]).astype(jnp.bfloat16)
            summed = jnp.dot(
                gather_table,
                inbound.reshape(slot_count, BR * front_width),
                preferred_element_type=jnp.float32,
            )
            summed = summed.reshape(local_nodes, order_size, front_width)
            upcoming = right_sides[height + 1]
            residual_list[front] = upcoming - summed
    answer = [[None] * levels]
    for height in range(levels - 1, -1, -1):
        front = 0
        if height == levels - 1:
            carried = lower_sols[front][height]
        else:
            destination, source, slot_code = routes[height]
            above_rows = (
                answer[front][height + 1].astype(jnp.bfloat16).reshape(local_rows, BR * front_width)
            )
            arrived = arrivals[front][height]
            outbound = jnp.where(
                (arrived >= 0)[:, None],
                above_rows[jnp.maximum(arrived, 0)],
                jnp.zeros((), jnp.bfloat16),
            )
            outbound = outbound.reshape(devices, capacity, BR * front_width)
            returned = lax.all_to_all(outbound, "snode", split_axis=0, concat_axis=0, tiled=True)
            block_rows = returned.reshape(slot_count, BR * front_width)[destination]
            block_rows = block_rows.reshape(local_nodes, per_node * BR, front_width)
            carried = lower_sols[front][height] - jnp.einsum(
                "skw,skr->swr", off_diagonal[height], block_rows, preferred_element_type=jnp.float32
            )
        result = jnp.einsum("swv,swr->svr", full_diag[height], carried, precision=precise)
        answer[front][height] = result
    stacked = [answer[0][height] for height in range(levels)]
    return jnp.stack(stacked, axis=0)


def solution(mesh):
    in_specs = (
        P(None, "snode", None, "rhs"),
        P(None, "snode", "rhs", None),
        P(None, "snode", None, None),
        P(None, "snode", None),
        P(None, "snode", None),
    )
    out_specs = P(None, "snode", None, "rhs")
    return jax.shard_map(
        on_device, mesh=mesh, in_specs=in_specs, out_specs=out_specs, check_vma=False
    )
```

profile of v0, /device:TPU:0, one launch (start us, length us, event | category | flops | bytes accessed | tf_op | source)
XLA Modules:
  0.0 184.4 jit_solution(8188241477674339573)
XLA Ops:
  2.8 7.3 %all-to-all-start = ((s32[8,1,32]{2,1,0:T(1,128)}), s32[8,1,32]{2,1,0:T(1,128)S(1)}, u32[]{:S(2)}, u32[]{:S(2)}) async-start(s32[8,1,32]{2,1,0:T(1,128)} %all_to_all.24), calls=%async_computation | async-start | bytes 8192 | tf_op jit(solution)/shard_map/all_to_all | solution.py:71
  11.1 7.2 %all-gather = f32[1,2,256,256]{3,2,1,0:T(8,128)S(1)} all-gather(f32[1,2,64,256]{3,2,1,0:T(8,128)S(1)} %get-tuple-element.9), channel_id=2, replica_groups=mesh['snode'=8,'rhs'=4] {'rhs'}, dimensions={2}, use_global_device_ids=true | all-gather | bytes 655360 | tf_op jit(solution)/shard_map/all_gather | solution.py:25
  19.1 1.6 fusion.20
  22.5 2.4 %gather_fusion = bf16[256,2048]{1,0:T(8,128)(2,1)} fusion(bf16[128,2048]{1,0:T(8,128)(2,1)S(1)} %reshape.482, s32[1024]{0:T(1024)S(1)} %pad_clamp_fusion.5), kind=kCustom, calls=%fused_computation | custom fusion | bytes 2098176 | tf_op jit(solution)/shard_map/gather | solution.py:66
  24.8 2.3 %broadcast_select_fusion.2 = bf16[8,32,2048]{2,1,0:T(8,128)(2,1)} fusion(bf16[8,32,2048]{2,1,0:T(8,128)(2,1)} %bitcast.99, pred[8,32]{1,0:T(8,128)(4,1)S(1)} %ge.43), kind=kLoop, calls=%fused_computation.20 | loop fusion | flops 524288 | bytes 2097408 | tf_op jit(solution)/shard_map/jit(_where)/select_n | solution.py:65
  27.2 6.0 %all-to-all-start.1 = ((bf16[8,32,2048]{2,1,0:T(8,128)(2,1)}), bf16[8,32,2048]{2,1,0:T(8,128)(2,1)}, u32[]{:S(2)}, u32[]{:S(2)}) async-start(bf16[8,32,2048]{2,1,0:T(8,128)(2,1)} %broadcast_select_fusion.2), calls=%async_computation.1 | async-start | bytes 2097152 | tf_op jit(solution)/shard_map/all_to_all | solution.py:70
  35.0 7.0 %all-gather.1 = f32[1,2,256,256]{3,2,1,0:T(8,128)S(1)} all-gather(f32[1,2,64,256]{3,2,1,0:T(8,128)S(1)} %get-tuple-element.11), channel_id=3, replica_groups=mesh['snode'=8,'rhs'=4] {'rhs'}, dimensions={2}, use_global_device_ids=true | all-gather | bytes 655360 | tf_op jit(solution)/shard_map/all_gather | solution.py:25
  43.3 16.2 %all-to-all-done.1 = bf16[8,32,2048]{2,1,0:T(8,128)(2,1)} async-done(((bf16[8,32,2048]{2,1,0:T(8,128)(2,1)}), bf16[8,32,2048]{2,1,0:T(8,128)(2,1)}, u32[]{:S(2)}, u32[]{:S(2)}) %all-to-all-start.1) | async-done | bytes 1048608 | tf_op jit(solution)/shard_map/all_to_all | solution.py:70
  59.5 3.6 %all-to-all-start.2 = ((s32[8,1,32]{2,1,0:T(1,128)}), s32[8,1,32]{2,1,0:T(1,128)S(1)}, u32[]{:S(2)}, u32[]{:S(2)}) async-start(s32[8,1,32]{2,1,0:T(1,128)} %all_to_all.27), calls=%async_computation.2 | async-start | bytes 8192 | tf_op jit(solution)/shard_map/all_to_all | solution.py:71
  63.2 1.5 fusion.30
  64.7 1.7 fusion.17
  69.2 2.4 %gather_fusion.1 = bf16[256,2048]{1,0:T(8,128)(2,1)} fusion(bf16[128,2048]{1,0:T(8,128)(2,1)S(1)} %reshape.485, s32[1024]{0:T(1024)S(1)} %pad_clamp_fusion.4), kind=kCustom, calls=%fused_computation.1 | custom fusion | bytes 2098176 | tf_op jit(solution)/shard_map/gather | solution.py:66
  71.5 2.3 %broadcast_select_fusion = bf16[8,32,2048]{2,1,0:T(8,128)(2,1)} fusion(bf16[8,32,2048]{2,1,0:T(8,128)(2,1)} %bitcast.100, pred[8,32]{1,0:T(8,128)(4,1)S(1)} %ge.47), kind=kLoop, calls=%fused_computation.18 | loop fusion | flops 524288 | bytes 2097408 | tf_op jit(solution)/shard_map/jit(_where)/select_n | solution.py:65
  73.9 6.0 %all-to-all-start.3 = ((bf16[8,32,2048]{2,1,0:T(8,128)(2,1)}), bf16[8,32,2048]{2,1,0:T(8,128)(2,1)}, u32[]{:S(2)}, u32[]{:S(2)}) async-start(bf16[8,32,2048]{2,1,0:T(8,128)(2,1)} %broadcast_select_fusion), calls=%async_computation.3 | async-start | bytes 2097152 | tf_op jit(solution)/shard_map/all_to_all | solution.py:70
  79.9 6.5 %all-gather.2 = f32[1,2,256,256]{3,2,1,0:T(8,128)S(1)} all-gather(f32[1,2,64,256]{3,2,1,0:T(8,128)S(1)} %get-tuple-element.10), channel_id=4, replica_groups=mesh['snode'=8,'rhs'=4] {'rhs'}, dimensions={2}, use_global_device_ids=true | all-gather | bytes 655360 | tf_op jit(solution)/shard_map/all_gather | solution.py:25
  87.2 18.4 %all-to-all-done.3 = bf16[8,32,2048]{2,1,0:T(8,128)(2,1)} async-done(((bf16[8,32,2048]{2,1,0:T(8,128)(2,1)}), bf16[8,32,2048]{2,1,0:T(8,128)(2,1)}, u32[]{:S(2)}, u32[]{:S(2)}) %all-to-all-start.3) | async-done | bytes 1048608 | tf_op jit(solution)/shard_map/all_to_all | solution.py:70
  105.6 1.5 fusion.31
  107.1 1.7 fusion.13
  112.7 3.7 %all-to-all-start.4 = ((bf16[8,32,2048]{2,1,0:T(8,128)(2,1)}), bf16[8,32,2048]{2,1,0:T(8,128)(2,1)S(1)}, u32[]{:S(2)}, u32[]{:S(2)}) async-start(bf16[8,32,2048]{2,1,0:T(8,128)(2,1)} %broadcast_select_fusion.1), calls=%async_computation.4 | async-start | bytes 2097152 | tf_op jit(solution)/shard_map/all_to_all | solution.py:101
  116.7 25.5 %all-to-all-done.4 = bf16[8,32,2048]{2,1,0:T(8,128)(2,1)S(1)} async-done(((bf16[8,32,2048]{2,1,0:T(8,128)(2,1)}), bf16[8,32,2048]{2,1,0:T(8,128)(2,1)S(1)}, u32[]{:S(2)}, u32[]{:S(2)}) %all-to-all-start.4) | async-done | bytes 1048608 | tf_op jit(solution)/shard_map/all_to_all | solution.py:101
  142.1 1.7 gather_fusion.3
  149.4 3.6 %all-to-all-start.5 = ((bf16[8,32,2048]{2,1,0:T(8,128)(2,1)}), bf16[8,32,2048]{2,1,0:T(8,128)(2,1)S(1)}, u32[]{:S(2)}, u32[]{:S(2)}) async-start(bf16[8,32,2048]{2,1,0:T(8,128)(2,1)} %broadcast_select_fusion.3), calls=%async_computation.5 | async-start | bytes 2097152 | tf_op jit(solution)/shard_map/all_to_all | solution.py:101
  153.1 25.8 %all-to-all-done.5 = bf16[8,32,2048]{2,1,0:T(8,128)(2,1)S(1)} async-done(((bf16[8,32,2048]{2,1,0:T(8,128)(2,1)}), bf16[8,32,2048]{2,1,0:T(8,128)(2,1)S(1)}, u32[]{:S(2)}, u32[]{:S(2)}) %all-to-all-start.5) | async-done | bytes 1048608 | tf_op jit(solution)/shard_map/all_to_all | solution.py:101
  178.9 1.7 gather_fusion.5
  (105 shorter events, 26.5 us)
Async XLA Ops:
  0.0 21.4 %copy-start = (bf16[2,2,1024,256]{3,2,1,0:T(8,128)(2,1)S(1)}, bf16[2,2,1024,256]{3,2,1,0:T(8,128)(2,1)}, u32[]{:S(2)}) copy-start(bf16[2,2,1024,256]{3,2,1,0:T(8,128)(2,1)} %param.7) | copy-start | bytes 6291460
  0.8 1.1 copy-start.9
  0.9 32.3 %copy-start.11 = (s32[1,2,64]{2,1,0:T(2,128)}, s32[1,2,64]{2,1,0:T(2,128)S(1)}, u32[]{:S(2)}) copy-start(s32[1,2,64]{2,1,0:T(2,128)S(1)} %get-tuple-element.12) | copy-start | bytes 1540
  1.9 16.4 %copy-start.13 = (s32[128]{0:T(128)}, s32[128]{0:T(128)S(1)}, u32[]{:S(2)}) copy-start(s32[128]{0:T(128)S(1)} %convert_reduce_fusion.1) | copy-start | bytes 1540
  2.8 24.4 %all-to-all-start = ((s32[8,1,32]{2,1,0:T(1,128)}), s32[8,1,32]{2,1,0:T(1,128)S(1)}, u32[]{:S(2)}, u32[]{:S(2)}) async-start(s32[8,1,32]{2,1,0:T(1,128)} %all_to_all.24), calls=%async_computation | async-start | bytes 8192 | tf_op jit(solution)/shard_map/all_to_all | solution.py:71
  18.3 0.8 copy-start.1
  20.7 0.7 copy-start.5
  27.2 32.4 %all-to-all-start.1 = ((bf16[8,32,2048]{2,1,0:T(8,128)(2,1)}), bf16[8,32,2048]{2,1,0:T(8,128)(2,1)}, u32[]{:S(2)}, u32[]{:S(2)}) async-start(bf16[8,32,2048]{2,1,0:T(8,128)(2,1)} %broadcast_select_fusion.2), calls=%async_computation.1 | async-start | bytes 2097152 | tf_op jit(solution)/shard_map/all_to_all | solution.py:70
  33.5 0.5 copy-start.15
  42.0 24.9 %copy-start.3 = (f32[1,2,256,256]{3,2,1,0:T(8,128)}, f32[1,2,256,256]{3,2,1,0:T(8,128)S(1)}, u32[]{:S(2)}) copy-start(f32[1,2,256,256]{3,2,1,0:T(8,128)S(1)} %all-gather.1) | copy-start | bytes 1572868
  59.5 14.3 %all-to-all-start.2 = ((s32[8,1,32]{2,1,0:T(1,128)}), s32[8,1,32]{2,1,0:T(1,128)S(1)}, u32[]{:S(2)}, u32[]{:S(2)}) async-start(s32[8,1,32]{2,1,0:T(1,128)} %all_to_all.27), calls=%async_computation.2 | async-start | bytes 8192 | tf_op jit(solution)/shard_map/all_to_all | solution.py:71
  73.9 31.7 %all-to-all-start.3 = ((bf16[8,32,2048]{2,1,0:T(8,128)(2,1)}), bf16[8,32,2048]{2,1,0:T(8,128)(2,1)}, u32[]{:S(2)}, u32[]{:S(2)}) async-start(bf16[8,32,2048]{2,1,0:T(8,128)(2,1)} %broadcast_select_fusion), calls=%async_computation.3 | async-start | bytes 2097152 | tf_op jit(solution)/shard_map/all_to_all | solution.py:70
  111.5 4.9 %copy-start.12 = (s32[1,2,64]{2,1,0:T(2,128)S(1)}, s32[1,2,64]{2,1,0:T(2,128)}, u32[]{:S(2)}) copy-start(s32[1,2,64]{2,1,0:T(2,128)} %copy-done.11) | copy-start | bytes 1540
  111.5 5.0 %copy-start.16 = (s32[128]{0:T(128)S(1)}, s32[128]{0:T(128)}, u32[]{:S(2)}) copy-start(s32[128]{0:T(128)} %copy-done.15) | copy-start | bytes 1540
  112.7 29.4 %all-to-all-start.4 = ((bf16[8,32,2048]{2,1,0:T(8,128)(2,1)}), bf16[8,32,2048]{2,1,0:T(8,128)(2,1)S(1)}, u32[]{:S(2)}, u32[]{:S(2)}) async-start(bf16[8,32,2048]{2,1,0:T(8,128)(2,1)} %broadcast_select_fusion.1), calls=%async_computation.4 | async-start | bytes 2097152 | tf_op jit(solution)/shard_map/all_to_all | solution.py:101
  143.8 1.7 copy-start.4
  148.3 4.7 %copy-start.10 = (s32[1,2,64]{2,1,0:T(2,128)S(1)}, s32[1,2,64]{2,1,0:T(2,128)}, u32[]{:S(2)}) copy-start(s32[1,2,64]{2,1,0:T(2,128)} %copy-done.9) | copy-start | bytes 1540
  148.3 4.8 %copy-start.14 = (s32[128]{0:T(128)S(1)}, s32[128]{0:T(128)}, u32[]{:S(2)}) copy-start(s32[128]{0:T(128)} %copy-done.13) | copy-start | bytes 1540
  149.4 29.5 %all-to-all-start.5 = ((bf16[8,32,2048]{2,1,0:T(8,128)(2,1)}), bf16[8,32,2048]{2,1,0:T(8,128)(2,1)S(1)}, u32[]{:S(2)}, u32[]{:S(2)}) async-start(bf16[8,32,2048]{2,1,0:T(8,128)(2,1)} %broadcast_select_fusion.3), calls=%async_computation.5 | async-start | bytes 2097152 | tf_op jit(solution)/shard_map/all_to_all | solution.py:101
  178.9 3.1 %copy-start.6 = (f32[2,256,128]{2,1,0:T(8,128)S(1)}, f32[2,256,128]{2,1,0:T(8,128)}, u32[]{:S(2)}) copy-start(f32[2,256,128]{2,1,0:T(8,128)} %copy-done.5) | copy-start | bytes 786436
  180.6 1.9 %copy-start.2 = (f32[1,2,256,256]{3,2,1,0:T(8,128)S(1)}, f32[1,2,256,256]{3,2,1,0:T(8,128)}, u32[]{:S(2)}) copy-start(f32[1,2,256,256]{3,2,1,0:T(8,128)} %copy-done.1) | copy-start | bytes 1572868
  182.0 1.2 copy-start.7
  182.0 1.2 copy-start.8
where the time goes:
time: 185 us; the launch traced here: 184 us
  waiting for transfers between devices  85.9 us (46%)
  starting transfers between devices  30.2 us (16%)
  local copies, waits for them, and re-layouts  25.5 us (14%)
  blocking collectives  20.7 us (11%)
  matrix products  12.7 us (7%)
  other arithmetic  9.06 us (5%)
    all_to_all x4, waiting for transfers between devices, on_device(): lax.all_to_all(outbound, 'snode', split_axis=0, concat_axis=0, tiled=True)  85.9 us
    all_gather x3, blocking collectives, on_device(): lax.all_gather(diag_inverse[height], 'rhs', axis=1, tiled=True)  20.7 us
    all_to_all x4, starting transfers between devices, on_device(): lax.all_to_all(outbound, 'snode', split_axis=0, concat_axis=0, tiled=True)  19.3 us
    all_to_all x2, starting transfers between devices, on_device(): lax.all_to_all(slot_code, 'snode', split_axis=0, concat_axis=0, tiled=True)  10.9 us
    dot_general x3, matrix products, on_device(): jnp.einsum('svw,swr->svr', full_diag[height], residual_list[front], preci...  4.88 us
    gather x2, local copies, waits for them, and re-layouts, on_device(): update[jnp.maximum(source, 0)]  4.71 us
    select_n x2, other arithmetic, on_device(): jnp.where((source >= 0)[:, None], update[jnp.maximum(source, 0)], jnp.zer...  4.69 us
  transfers between devices with their start and end apart: 6, of which 4 were waited for; matrix products, arithmetic and copies ran while one was open for 12% of the time, Pallas kernels for 0%

commit v1 on v0

--- a/solution.py
+++ b/solution.py
@@ -1,6 +1,10 @@
+import functools
+
 import jax
 import jax.numpy as jnp
 from jax import lax
+from jax.experimental import pallas as pl
+from jax.experimental.pallas import tpu as pltpu
 from jax.sharding import PartitionSpec as P
 
 BR = 16
@@ -110,6 +114,302 @@
     return jnp.stack(stacked, axis=0)
 
 
+MESH = pl.DeviceIdType.MESH
+PAIR = 2
+
+
+def mm(a, b):
+    return jnp.dot(a, b, preferred_element_type=jnp.float32)
+
+
+def split(a):
+    high = a.astype(jnp.bfloat16)
+    return high, (a - high.astype(jnp.float32)).astype(jnp.bfloat16)
+
+
+def mm3(a_high, a_low, b):
+    cols = b.shape[1]
+    b_high, b_low = split(b)
+    wide = mm(a_high, jnp.concatenate([b_high, b_low], axis=1))
+    return wide[:, :cols] + wide[:, cols:] + mm(a_low, b_high)
+
+
+def dense_kernel(
+    n, parts, rs_ref, dg_ref, od_ref, codev_ref, codes_ref, out_ref,
+    full, diag_t, od_t, low, upd, nat, part, rx, ru, rd, zs, above, picked,
+    dsend, drecv, xsend, xrecv, zsend, urecv, drecv2, asend, arecv, bsend, brecv,
+):
+    levels, local, order, cols = rs_ref.shape
+    shard = dg_ref.shape[2]
+    outgoing = codev_ref.shape[2]
+    per_node = outgoing // local
+    local_rows = local * order // BR
+    line = n // PAIR
+    ymany = parts // PAIR
+    me = lax.axis_index("snode")
+    z, x = me // PAIR, me % PAIR
+    mine = lax.axis_index("rhs")
+    yy, cc = mine // PAIR, mine % PAIR
+    mate = {"snode": z * PAIR + (1 - x)}
+    over = {"snode": (z + 1) * PAIR + x}
+    under = {"snode": (z - 1) * PAIR + x}
+    twin = {"rhs": yy * PAIR + (1 - cc)}
+    sides = [(yy + k) % ymany for k in range(1, ymany)]
+
+    def remote(src, dst, s_sem, r_sem, where):
+        return pltpu.make_async_remote_copy(
+            src_ref=src, dst_ref=dst, send_sem=s_sem, recv_sem=r_sem,
+            device_id=where, device_id_type=MESH,
+        )
+
+    barrier = pltpu.get_barrier_semaphore()
+
+    def greet(where):
+        pl.semaphore_signal(barrier, inc=1, device_id=where, device_id_type=MESH)
+
+    greet(mate)
+    greet(twin)
+    for side in sides:
+        greet({"rhs": side * PAIR + cc})
+
+    @pl.when(z > 0)
+    def _():
+        greet(under)
+
+    @pl.when(z < line - 1)
+    def _():
+        greet(over)
+
+    ends = jnp.where(z > 0, 1, 0) + jnp.where(z < line - 1, 1, 0)
+    pl.semaphore_wait(barrier, 1 + ymany + ends)
+
+    sent = []
+    gather = []
+    for h in range(levels):
+        near = []
+        for k, side in enumerate(sides):
+            copy = remote(dg_ref.at[h], full.at[h, mine], dsend.at[h, k], drecv.at[h, k],
+                          {"rhs": side * PAIR + cc})
+            copy.start()
+            near.append(copy)
+        own = remote(dg_ref.at[h], full.at[h, mine], dsend.at[h, ymany], drecv.at[h, ymany], twin)
+        own.start()
+        gather.append((near, own))
+    for h in range(levels):
+        full[h, mine] = dg_ref[h]
+
+    def finish_gather(h):
+        near, own = gather[h]
+        hops = []
+        for k, copy in enumerate(near):
+            copy.wait_recv()
+            origin = ((yy + ymany - 1 - k) % ymany) * PAIR + cc
+            hop = remote(full.at[h, origin], full.at[h, origin], dsend.at[h, ymany + 1 + k],
+                         drecv.at[h, ymany + 1 + k], twin)
+            hop.start()
+            hops.append(hop)
+        own.wait_recv()
+        for hop in hops:
+            hop.wait_recv()
+        sent.extend(near + [own] + hops)
+
+    def diag(h, s):
+        return full[h, :, s].reshape(order, order)
+
+    def forward(h, s, residual):
+        high, low_part = split(diag(h, s))
+        low[h, s] = mm3(high, low_part, residual)
+
+    def backward(h, s, carried):
+        out_ref[h, s] = mm3(diag_t[h, s, 0], diag_t[h, s, 1], carried)
+
+    def prepare(h):
+        for s in range(local):
+            high, low_part = split(diag(h, s).T)
+            diag_t[h, s, 0] = high
+            diag_t[h, s, 1] = low_part
+
+    finish_gather(0)
+    for s in range(local):
+        forward(0, s, rs_ref[0, s])
+
+    for h in range(levels - 1):
+        for s in range(local):
+            upd[pl.ds(s * per_node * BR, per_node * BR), :] = mm(
+                od_ref[h, s], low[h, s].astype(jnp.bfloat16)
+            )
+        rows = lax.broadcasted_iota(jnp.int32, (n * local_rows, outgoing), 0)
+        table = jnp.where(rows == codev_ref[h], 1.0, 0.0).astype(jnp.bfloat16)
+        for r in range(BR):
+            piece = upd[pl.ds(r, outgoing, stride=BR), :].astype(jnp.bfloat16)
+            summed = mm(table, piece).astype(jnp.bfloat16)
+            for d in range(n):
+                part[h, d, r * local_rows:(r + 1) * local_rows, :] = (
+                    summed[d * local_rows:(d + 1) * local_rows]
+                )
+
+        for zz in range(line):
+            @pl.when(z == zz)
+            def _(zz=zz):
+                for d in sorted(range(line), key=lambda d: -abs(d - zz)):
+                    remote(part.at[h, d * PAIR + (1 - x)], rx.at[h, d], xsend.at[h, d],
+                           xrecv.at[h, d], mate).start()
+
+        if h == 0:
+            for later in range(1, levels):
+                finish_gather(later)
+        prepare(h)
+        if h == levels - 2:
+            prepare(levels - 1)
+        for s in range(local):
+            od_t[h, s] = od_ref[h, s].T
+
+        for zz in range(line):
+            @pl.when(z == zz)
+            def _(zz=zz):
+                for d in sorted(range(line), key=lambda d: -abs(d - zz)):
+                    remote(part.at[h, d * PAIR + (1 - x)], rx.at[h, d], xsend.at[h, d],
+                           xrecv.at[h, d], mate).wait_recv()
+                    total = part[h, d * PAIR + x].astype(jnp.float32) + rx[h, d].astype(jnp.float32)
+                    if d >= zz and zz > 0:
+                        remote(zs.at[h, d], ru.at[h, d], zsend.at[h, d], urecv.at[h, d],
+                               under).wait_recv()
+                        total = total + ru[h, d].astype(jnp.float32)
+                    if d <= zz and zz < line - 1:
+                        remote(zs.at[h, d], rd.at[h, d], zsend.at[h, d], drecv2.at[h, d],
+                               over).wait_recv()
+                        total = total + rd[h, d].astype(jnp.float32)
+                    if d != zz:
+                        zs[h, d] = total.astype(jnp.bfloat16)
+                    if d > zz:
+                        remote(zs.at[h, d], ru.at[h, d], zsend.at[h, d], urecv.at[h, d],
+                               over).start()
+                    elif d < zz:
+                        remote(zs.at[h, d], rd.at[h, d], zsend.at[h, d], drecv2.at[h, d],
+                               under).start()
+                    else:
+                        for r in range(BR):
+                            nat[pl.ds(r, local_rows, stride=BR), :] = (
+                                total[r * local_rows:(r + 1) * local_rows]
+                            )
+        for s in range(local):
+            forward(h + 1, s, rs_ref[h + 1, s] - nat[pl.ds(s * order, order), :])
+
+    for s in range(local):
+        backward(levels - 1, s, low[levels - 1, s])
+
+    for h in range(levels - 2, -1, -1):
+        above[h][me] = out_ref[h + 1].reshape(local_rows, BR, cols).astype(jnp.bfloat16)
+
+        def hop(s, where, sem_s, sem_r, col):
+            slot = above[h].at[s * PAIR + col]
+            return remote(slot, slot, sem_s, sem_r, where)
+
+        for zz in range(line):
+            @pl.when(z == zz)
+            def _(zz=zz):
+                for s in sorted(range(line), key=lambda s: abs(s - zz)):
+                    if s != zz:
+                        hop(s, mate, asend.at[h, 0, s], arecv.at[h, s], x).wait_recv()
+                    if s <= zz and zz < line - 1:
+                        hop(s, over, asend.at[h, 0, s], arecv.at[h, s], x).start()
+                    if s >= zz and zz > 0:
+                        hop(s, under, asend.at[h, 1, s], arecv.at[h, s], x).start()
+                    hop(s, mate, bsend.at[h, s], brecv.at[h, s], x).start()
+        for s in range(line):
+            hop(s, mate, bsend.at[h, s], brecv.at[h, s], 1 - x).wait_recv()
+        for k in range(outgoing):
+            picked[pl.ds(k * BR, BR), :] = above[h][
+                codes_ref[h, k] // local_rows, codes_ref[h, k] % local_rows
+            ]
+        for s in range(local):
+            carried = low[h, s] - mm(
+                od_t[h, s], picked[pl.ds(s * per_node * BR, per_node * BR), :]
+            )
+            backward(h, s, carried)
+
+    for copy in sent:
+        copy.wait_send()
+    for h in range(levels - 1):
+        for d in range(line):
+            remote(part.at[h, d * PAIR + (1 - x)], rx.at[h, d], xsend.at[h, d],
+                   xrecv.at[h, d], mate).wait_send()
+            slot = above[h].at[d * PAIR + x]
+            remote(slot, slot, bsend.at[h, d], brecv.at[h, d], mate).wait_send()
+        for zz in range(line):
+            @pl.when(z == zz)
+            def _(zz=zz):
+                for d in range(line):
+                    slot = above[h].at[d * PAIR + x]
+                    if d != zz:
+                        remote(zs.at[h, d], ru.at[h, d], zsend.at[h, d], urecv.at[h, d],
+                               mate).wait_send()
+                    if d <= zz and zz < line - 1:
+                        remote(slot, slot, asend.at[h, 0, d], arecv.at[h, d], mate).wait_send()
+                    if d >= zz and zz > 0:
+                        remote(slot, slot, asend.at[h, 1, d], arecv.at[h, d], mate).wait_send()
+
+
+def dense_on_device(right_sides, diag_inverse, off_diagonal, target_snode, target_block):
+    levels, local, order, cols = right_sides.shape
+    n, parts = lax.axis_size("snode"), lax.axis_size("rhs")
+    outgoing = local * target_snode.shape[2]
+    row_blocks = order // BR
+    local_rows = local * row_blocks
+    chunk = local_rows * BR
+    line = n // PAIR
+    ymany = parts // PAIR
+    code = (target_snode * row_blocks + target_block).reshape(levels - 1, outgoing)
+    bf, f32 = jnp.bfloat16, jnp.float32
+    steps = levels - 1
+    dma = pltpu.SemaphoreType.DMA
+    whole = pl.BlockSpec(memory_space=pltpu.VMEM)
+    return pl.pallas_call(
+        functools.partial(dense_kernel, n, parts),
+        out_shape=jax.ShapeDtypeStruct(right_sides.shape, f32),
+        in_specs=[whole] * 4 + [pl.BlockSpec(memory_space=pltpu.SMEM)],
+        out_specs=whole,
+        scratch_shapes=[
+            pltpu.VMEM((levels, parts) + diag_inverse.shape[1:], f32),
+            pltpu.VMEM((levels, local, 2, order, order), bf),
+            pltpu.VMEM((steps, local, order, off_diagonal.shape[2]), bf),
+            pltpu.VMEM(right_sides.shape, f32),
+            pltpu.VMEM((outgoing * BR, cols), f32),
+            pltpu.VMEM((chunk, cols), f32),
+            pltpu.VMEM((steps, n, chunk, cols), bf),
+            pltpu.VMEM((steps, line, chunk, cols), bf),
+            pltpu.VMEM((steps, line, chunk, cols), bf),
+            pltpu.VMEM((steps, line, chunk, cols), bf),
+            pltpu.VMEM((steps, line, chunk, cols), bf),
+            [pltpu.VMEM((n, local_rows, BR, cols), bf)] * steps,
+            pltpu.VMEM((outgoing * BR, cols), bf),
+            dma((levels, 2 * ymany)),
+            dma((levels, 2 * ymany)),
+            dma((steps, line)),
+            dma((steps, line)),
+            dma((steps, line)),
+            dma((steps, line)),
+            dma((steps, line)),
+            dma((steps, 2, line)),
+            dma((steps, line)),
+            dma((steps, line)),
+            dma((steps, line)),
+        ],
+        compiler_params=pltpu.CompilerParams(
+            collective_id=0, has_side_effects=True, vmem_limit_bytes=48 * 1024 * 1024
+        ),
+    )(right_sides, diag_inverse, off_diagonal, code.reshape(steps, 1, outgoing), code)
+
+
+def program(right_sides, diag_inverse, off_diagonal, target_snode, target_block):
+    n, parts = lax.axis_size("snode"), lax.axis_size("rhs")
+    capacity = 2 * right_sides.shape[1] * target_snode.shape[2] // n
+    local_rows = right_sides.shape[1] * right_sides.shape[2] // BR
+    dense = capacity >= local_rows and n % PAIR == 0 and parts % PAIR == 0
+    body = dense_on_device if dense else on_device
+    return body(right_sides, diag_inverse, off_diagonal, target_snode, target_block)
+
+
 def solution(mesh):
     in_specs = (
         P(None, "snode", None, "rhs"),
@@ -120,5 +420,5 @@
     )
     out_specs = P(None, "snode", None, "rhs")
     return jax.shard_map(
-        on_device, mesh=mesh, in_specs=in_specs, out_specs=out_specs, check_vma=False
+        program, mesh=mesh, in_specs=in_specs, out_specs=out_specs, check_vma=False
     )

time: 185 us -> 96.5 us (0.52)
  Pallas kernels: 0 us -> 90.8 us
  waiting for transfers between devices: 85.9 us -> 0 us
  starting transfers between devices: 30.2 us -> 0 us
  local copies, waits for them, and re-layouts: 25.5 us -> 4.76 us
  blocking collectives: 20.7 us -> 0 us
  matrix products: 12.7 us -> 0 us
  other arithmetic: 9.06 us -> 0.7 us
    pallas_call x0 -> x1, Pallas kernels: none -> 90.8 us  [dense_on_device(): pl.pallas_call(functools.partial(dense_kernel, n, parts), out_shape=jax.S...]
    all_to_all x6 -> x0, waiting for transfers between devices: 85.9 us -> none  [the longest x4 85.9 us: on_device(): lax.all_to_all(outbound, 'snode', split_axis=0, concat_axis=0, tiled=True)]
    all_to_all x6 -> x0, starting transfers between devices: 30.2 us -> none  [the longest x4 19.3 us: on_device(): lax.all_to_all(outbound, 'snode', split_axis=0, concat_axis=0, tiled=True)]
    all_gather x3 -> x0, blocking collectives: 20.7 us -> none  [on_device(): lax.all_gather(diag_inverse[height], 'rhs', axis=1, tiled=True)]
    dot_general x12 -> x0, matrix products: 12.7 us -> none  [the longest x3 4.88 us: on_device(): jnp.einsum('svw,swr->svr', full_diag[height], residual_list[front], preci...]
    gather x6 -> x0, local copies, waits for them, and re-layouts: 10.9 us -> none  [the longest x2 4.71 us: on_device(): update[jnp.maximum(source, 0)]]
    select_n x8 -> x0, other arithmetic: 7 us -> none  [the longest x2 4.69 us: on_device(): jnp.where((source >= 0)[:, None], update[jnp.maximum(source, 0)], jnp.zer...]
    reshape x8 -> x1, local copies, waits for them, and re-layouts: 4.4 us -> 0.08 us  [dense_on_device(): (target_snode * row_blocks + target_block).reshape(levels - 1, outgoing)]
  transfers between devices with their start and end apart: 6 -> 0, of which waited for: 4 -> 0; matrix products, arithmetic and copies ran while one was open for 12% -> 0% of each run, Pallas kernels for 0% -> 0%
where the time goes in v1:
time: 96.5 us; the launch traced here: 96.3 us
  Pallas kernels  90.8 us (94%)
  local copies, waits for them, and re-layouts  4.76 us (5%)
    pallas_call x1, Pallas kernels, dense_on_device(): pl.pallas_call(functools.partial(dense_kernel, n, parts), out_shape=jax.S...  90.8 us
    unnamed x7, local copies, waits for them, and re-layouts  4.6 us

profile of v1, /device:TPU:0, one launch (start us, length us, event | category | flops | bytes accessed | tf_op | source)
XLA Modules:
  0.0 96.3 jit_solution(1980010104901206462)
XLA Ops:
  0.0 0.7 multiply_add_fusion
  0.7 0.1 reshape.3.codes_ref
  0.8 0.1 reshape_reshape.3.codev_ref
  0.9 0.0 copy-start
  0.9 1.6 %copy-done = bf16[2,2,1024,256]{3,2,1,0:T(8,128)(2,1)S(1)} copy-done((bf16[2,2,1024,256]{3,2,1,0:T(8,128)(2,1)S(1)}, bf16[2,2,1024,256]{3,2,1,0:T(8,128)(2,1)}, u32[]{:S(2)}) %copy-start) | copy-done | bytes 2097176
  2.5 0.0 copy-start.1
  2.5 1.1 %copy-done.1 = f32[3,2,256,128]{3,2,1,0:T(8,128)S(1)} copy-done((f32[3,2,256,128]{3,2,1,0:T(8,128)S(1)}, f32[3,2,256,128]{3,2,1,0:T(8,128)}, u32[]{:S(2)}) %copy-start.1) | copy-done | bytes 786456
  3.6 0.0 copy-start.2
  3.6 1.0 %copy-done.2 = f32[3,2,64,256]{3,2,1,0:T(8,128)S(1)} copy-done((f32[3,2,64,256]{3,2,1,0:T(8,128)S(1)}, f32[3,2,64,256]{3,2,1,0:T(8,128)}, u32[]{:S(2)}) %copy-start.2) | copy-done | bytes 393240
  4.6 90.8 %shard_map.55 = f32[3,2,256,128]{3,2,1,0:T(8,128)S(1)} custom-call(f32[3,2,256,128]{3,2,1,0:T(8,128)S(1)} %copy-done.1, f32[3,2,64,256]{3,2,1,0:T(8,128)S(1)} %copy-done.2, bf16[2,2,1024,256]{3,2,1,0:T(8,128)(2,1)S(1)} %copy-done, s32[2,1,128]{2,1,0:T(1,128)S(1)} %reshape_reshape.3.codev_ref, s32[2,128]{1,0:T(2,128)S(1)} %reshape.3.codes_ref), custom_call_target="tpu_custom_call" | custom-call | tf_op jit(solution)/shard_map/pallas_call | solution.py:367
  95.4 0.9 copy.7
Async XLA Ops:
  0.9 1.6 %copy-start = (bf16[2,2,1024,256]{3,2,1,0:T(8,128)(2,1)S(1)}, bf16[2,2,1024,256]{3,2,1,0:T(8,128)(2,1)}, u32[]{:S(2)}) copy-start(bf16[2,2,1024,256]{3,2,1,0:T(8,128)(2,1)} %od_ref.1) | copy-start | bytes 6291460
  2.5 1.1 %copy-start.1 = (f32[3,2,256,128]{3,2,1,0:T(8,128)S(1)}, f32[3,2,256,128]{3,2,1,0:T(8,128)}, u32[]{:S(2)}) copy-start(f32[3,2,256,128]{3,2,1,0:T(8,128)} %rs_ref.1) | copy-start | bytes 2359300
  3.6 1.0 %copy-start.2 = (f32[3,2,64,256]{3,2,1,0:T(8,128)S(1)}, f32[3,2,64,256]{3,2,1,0:T(8,128)}, u32[]{:S(2)}) copy-start(f32[3,2,64,256]{3,2,1,0:T(8,128)} %dg_ref.1) | copy-start | bytes 1179652

commit v2 on v1

--- a/solution.py
+++ b/solution.py
@@ -135,17 +135,19 @@
 
 
 def dense_kernel(
-    n, parts, rs_ref, dg_ref, od_ref, codev_ref, codes_ref, out_ref,
-    full, diag_t, od_t, low, upd, nat, part, rx, ru, rd, zs, above, picked,
-    dsend, drecv, xsend, xrecv, zsend, urecv, drecv2, asend, arecv, bsend, brecv,
+    n, parts, rs_hbm, dg_ref, od_hbm, snode_v, block_v, snode_s, block_s, out_hbm,
+    full, diag_t, od_ref, od_t, rs_ref, low, sol, upd, nat, part, rx, ru, rd, zs, above, picked,
+    lsend, osend, dsend, drecv, xsend, xrecv, zsend, urecv, wrecv, asend, arecv, bsend, brecv,
 ):
     levels, local, order, cols = rs_ref.shape
-    shard = dg_ref.shape[2]
-    outgoing = codev_ref.shape[2]
-    per_node = outgoing // local
-    local_rows = local * order // BR
+    per_node = snode_v.shape[2]
+    outgoing = local * per_node
+    row_blocks = order // BR
+    local_rows = local * row_blocks
     line = n // PAIR
     ymany = parts // PAIR
+    cut = local
+    width = BR // cut
     me = lax.axis_index("snode")
     z, x = me // PAIR, me % PAIR
     mine = lax.axis_index("rhs")
@@ -180,12 +182,29 @@
     def _():
         greet(over)
 
+    own_diag = [
+        pltpu.make_async_copy(dg_ref.at[h], full.at[h, mine], lsend.at[0, h])
+        for h in range(levels)
+    ]
+    load_rs = [
+        pltpu.make_async_copy(rs_hbm.at[h], rs_ref.at[h], lsend.at[1, h]) for h in range(levels)
+    ]
+    load_od = [
+        pltpu.make_async_copy(od_hbm.at[h], od_ref.at[h], lsend.at[2, h])
+        for h in range(levels - 1)
+    ]
+    for h in range(levels):
+        own_diag[h].start()
+        load_rs[h].start()
+        if h < levels - 1:
+            load_od[h].start()
+
     ends = jnp.where(z > 0, 1, 0) + jnp.where(z < line - 1, 1, 0)
     pl.semaphore_wait(barrier, 1 + ymany + ends)
 
     sent = []
-    gather = []
-    for h in range(levels):
+
+    def start_gather(h):
         near = []
         for k, side in enumerate(sides):
             copy = remote(dg_ref.at[h], full.at[h, mine], dsend.at[h, k], drecv.at[h, k],
@@ -194,12 +213,9 @@
             near.append(copy)
         own = remote(dg_ref.at[h], full.at[h, mine], dsend.at[h, ymany], drecv.at[h, ymany], twin)
         own.start()
-        gather.append((near, own))
-    for h in range(levels):
-        full[h, mine] = dg_ref[h]
-
-    def finish_gather(h):
-        near, own = gather[h]
+        return near, own
+
+    def finish_gather(h, near, own):
         hops = []
         for k, copy in enumerate(near):
             copy.wait_recv()
@@ -209,6 +225,7 @@
             hop.start()
             hops.append(hop)
         own.wait_recv()
+        own_diag[h].wait()
         for hop in hops:
             hop.wait_recv()
         sent.extend(near + [own] + hops)
@@ -221,7 +238,7 @@
         low[h, s] = mm3(high, low_part, residual)
 
     def backward(h, s, carried):
-        out_ref[h, s] = mm3(diag_t[h, s, 0], diag_t[h, s, 1], carried)
+        sol[h, s] = mm3(diag_t[h, s, 0], diag_t[h, s, 1], carried)
 
     def prepare(h):
         for s in range(local):
@@ -229,125 +246,191 @@
             diag_t[h, s, 0] = high
             diag_t[h, s, 1] = low_part
 
-    finish_gather(0)
+    def turn(h):
+        for s in range(local):
+            od_t[h, s] = od_ref[h, s].T
+
+    def codes(h):
+        code = snode_v[h] * row_blocks + block_v[h]
+        return jnp.concatenate([code[s:s + 1] for s in range(local)], axis=1)
+
+    def by_line(body):
+        for zz in range(line):
+            @pl.when(z == zz)
+            def _(zz=zz):
+                body(zz)
+
+    def x_copy(h, q, d):
+        return remote(part.at[h, q, d * PAIR + (1 - x)], rx.at[h, q, d], xsend.at[h, q, d],
+                      xrecv.at[h, q, d], mate)
+
+    def up_copy(h, q, d, where):
+        return remote(zs.at[h, q, d], ru.at[h, q, d], zsend.at[h, q, d], urecv.at[h, q, d], where)
+
+    def down_copy(h, q, d, where):
+        return remote(zs.at[h, q, d], rd.at[h, q, d], zsend.at[h, q, d], wrecv.at[h, q, d], where)
+
+    def far_first(zz):
+        return sorted(range(line), key=lambda d: -abs(d - zz))
+
+    first = start_gather(0)
+    tables = []
+    rows = lax.broadcasted_iota(jnp.int32, (n * local_rows, outgoing), 0)
+    for h in range(levels - 1):
+        tables.append(jnp.where(rows == codes(h), 1.0, 0.0).astype(jnp.bfloat16))
+    finish_gather(0, *first)
+    gather = [None] + [start_gather(h) for h in range(1, levels)]
+    load_rs[0].wait()
     for s in range(local):
         forward(0, s, rs_ref[0, s])
 
     for h in range(levels - 1):
+        load_od[h].wait()
         for s in range(local):
             upd[pl.ds(s * per_node * BR, per_node * BR), :] = mm(
                 od_ref[h, s], low[h, s].astype(jnp.bfloat16)
             )
-        rows = lax.broadcasted_iota(jnp.int32, (n * local_rows, outgoing), 0)
-        table = jnp.where(rows == codev_ref[h], 1.0, 0.0).astype(jnp.bfloat16)
-        for r in range(BR):
-            piece = upd[pl.ds(r, outgoing, stride=BR), :].astype(jnp.bfloat16)
-            summed = mm(table, piece).astype(jnp.bfloat16)
-            for d in range(n):
-                part[h, d, r * local_rows:(r + 1) * local_rows, :] = (
-                    summed[d * local_rows:(d + 1) * local_rows]
-                )
-
-        for zz in range(line):
-            @pl.when(z == zz)
-            def _(zz=zz):
-                for d in sorted(range(line), key=lambda d: -abs(d - zz)):
-                    remote(part.at[h, d * PAIR + (1 - x)], rx.at[h, d], xsend.at[h, d],
-                           xrecv.at[h, d], mate).start()
+        for q in range(cut):
+            for r in range(width):
+                piece = upd[pl.ds(q * width + r, outgoing, stride=BR), :].astype(jnp.bfloat16)
+                summed = mm(tables[h], piece).astype(jnp.bfloat16)
+                for d in range(n):
+                    part[h, q, d, r * local_rows:(r + 1) * local_rows, :] = (
+                        summed[d * local_rows:(d + 1) * local_rows]
+                    )
+
+            def send_x(zz, q=q, h=h):
+                for d in far_first(zz):
+                    x_copy(h, q, d).start()
+
+            by_line(send_x)
 
         if h == 0:
-            for later in range(1, levels):
-                finish_gather(later)
-        prepare(h)
+            prepare(0)
+            turn(0)
         if h == levels - 2:
-            prepare(levels - 1)
-        for s in range(local):
-            od_t[h, s] = od_ref[h, s].T
-
-        for zz in range(line):
-            @pl.when(z == zz)
-            def _(zz=zz):
-                for d in sorted(range(line), key=lambda d: -abs(d - zz)):
-                    remote(part.at[h, d * PAIR + (1 - x)], rx.at[h, d], xsend.at[h, d],
-                           xrecv.at[h, d], mate).wait_recv()
-                    total = part[h, d * PAIR + x].astype(jnp.float32) + rx[h, d].astype(jnp.float32)
+            for later in range(max(h + 1, 2), levels):
+                finish_gather(later, *gather[later])
+                prepare(later)
+
+        for q in range(cut):
+            def reduce(zz, q=q, h=h):
+                for d in far_first(zz):
+                    x_copy(h, q, d).wait_recv()
+                    total = (part[h, q, d * PAIR + x].astype(jnp.float32)
+                             + rx[h, q, d].astype(jnp.float32))
                     if d >= zz and zz > 0:
-                        remote(zs.at[h, d], ru.at[h, d], zsend.at[h, d], urecv.at[h, d],
-                               under).wait_recv()
-                        total = total + ru[h, d].astype(jnp.float32)
+                        up_copy(h, q, d, under).wait_recv()
+                        total = total + ru[h, q, d].astype(jnp.float32)
                     if d <= zz and zz < line - 1:
-                        remote(zs.at[h, d], rd.at[h, d], zsend.at[h, d], drecv2.at[h, d],
-                               over).wait_recv()
-                        total = total + rd[h, d].astype(jnp.float32)
+                        down_copy(h, q, d, over).wait_recv()
+                        total = total + rd[h, q, d].astype(jnp.float32)
                     if d != zz:
-                        zs[h, d] = total.astype(jnp.bfloat16)
+                        zs[h, q, d] = total.astype(jnp.bfloat16)
                     if d > zz:
-                        remote(zs.at[h, d], ru.at[h, d], zsend.at[h, d], urecv.at[h, d],
-                               over).start()
+                        up_copy(h, q, d, over).start()
                     elif d < zz:
-                        remote(zs.at[h, d], rd.at[h, d], zsend.at[h, d], drecv2.at[h, d],
-                               under).start()
+                        down_copy(h, q, d, under).start()
                     else:
-                        for r in range(BR):
-                            nat[pl.ds(r, local_rows, stride=BR), :] = (
+                        for r in range(width):
+                            nat[pl.ds(q * width + r, local_rows, stride=BR), :] = (
                                 total[r * local_rows:(r + 1) * local_rows]
                             )
+
+            by_line(reduce)
+            if h == 0 and q == 0:
+                finish_gather(1, *gather[1])
+        load_rs[h + 1].wait()
         for s in range(local):
             forward(h + 1, s, rs_ref[h + 1, s] - nat[pl.ds(s * order, order), :])
 
+    stores = []
+
+    def store(h):
+        copy = pltpu.make_async_copy(sol.at[h], out_hbm.at[h], osend.at[h])
+        copy.start()
+        stores.append(copy)
+
+    def hop(h, q, s, where, s_sem, r_sem, col):
+        slot = above[h].at[s * PAIR + col, pl.ds(q * row_blocks, row_blocks)]
+        return remote(slot, slot, s_sem, r_sem, where)
+
+    def line_hop(h, q, s, where, way):
+        return hop(h, q, s, where, asend.at[h, way, q, s], arecv.at[h, q, s], x)
+
+    def mate_hop(h, q, s, col):
+        return hop(h, q, s, mate, bsend.at[h, q, s], brecv.at[h, q, s], col)
+
+    def pass_on(h, q, s, zz):
+        if s <= zz and zz < line - 1:
+            line_hop(h, q, s, over, 0).start()
+        if s >= zz and zz > 0:
+            line_hop(h, q, s, under, 1).start()
+        mate_hop(h, q, s, x).start()
+
+    def publish(h, q):
+        above[h][me, q * row_blocks:(q + 1) * row_blocks] = (
+            sol[h + 1, q].reshape(row_blocks, BR, cols).astype(jnp.bfloat16)
+        )
+        by_line(lambda zz: pass_on(h, q, zz, zz))
+
     for s in range(local):
         backward(levels - 1, s, low[levels - 1, s])
+        publish(levels - 2, s)
+    store(levels - 1)
 
     for h in range(levels - 2, -1, -1):
-        above[h][me] = out_ref[h + 1].reshape(local_rows, BR, cols).astype(jnp.bfloat16)
-
-        def hop(s, where, sem_s, sem_r, col):
-            slot = above[h].at[s * PAIR + col]
-            return remote(slot, slot, sem_s, sem_r, where)
-
-        for zz in range(line):
-            @pl.when(z == zz)
-            def _(zz=zz):
-                for s in sorted(range(line), key=lambda s: abs(s - zz)):
+        if h > 0:
+            turn(h)
+            prepare(h)
+
+        def spread(zz, h=h):
+            for s in sorted(range(line), key=lambda s: abs(s - zz)):
+                for q in range(cut):
                     if s != zz:
-                        hop(s, mate, asend.at[h, 0, s], arecv.at[h, s], x).wait_recv()
-                    if s <= zz and zz < line - 1:
-                        hop(s, over, asend.at[h, 0, s], arecv.at[h, s], x).start()
-                    if s >= zz and zz > 0:
-                        hop(s, under, asend.at[h, 1, s], arecv.at[h, s], x).start()
-                    hop(s, mate, bsend.at[h, s], brecv.at[h, s], x).start()
+                        line_hop(h, q, s, over, 0).wait_recv()
+                        pass_on(h, q, s, zz)
+
+        by_line(spread)
         for s in range(line):
-            hop(s, mate, bsend.at[h, s], brecv.at[h, s], 1 - x).wait_recv()
-        for k in range(outgoing):
-            picked[pl.ds(k * BR, BR), :] = above[h][
-                codes_ref[h, k] // local_rows, codes_ref[h, k] % local_rows
-            ]
+            for q in range(cut):
+                mate_hop(h, q, s, 1 - x).wait_recv()
         for s in range(local):
+            for k in range(per_node):
+                picked[pl.ds((s * per_node + k) * BR, BR), :] = above[h][
+                    snode_s[h, s, k] // local,
+                    snode_s[h, s, k] % local * row_blocks + block_s[h, s, k],
+                ]
             carried = low[h, s] - mm(
                 od_t[h, s], picked[pl.ds(s * per_node * BR, per_node * BR), :]
             )
             backward(h, s, carried)
+            if h > 0:
+                publish(h - 1, s)
+        store(h)
 
     for copy in sent:
         copy.wait_send()
     for h in range(levels - 1):
-        for d in range(line):
-            remote(part.at[h, d * PAIR + (1 - x)], rx.at[h, d], xsend.at[h, d],
-                   xrecv.at[h, d], mate).wait_send()
-            slot = above[h].at[d * PAIR + x]
-            remote(slot, slot, bsend.at[h, d], brecv.at[h, d], mate).wait_send()
-        for zz in range(line):
-            @pl.when(z == zz)
-            def _(zz=zz):
+        for q in range(cut):
+            for d in range(line):
+                x_copy(h, q, d).wait_send()
+                mate_hop(h, q, d, x).wait_send()
+
+    def drain(zz):
+        for h in range(levels - 1):
+            for q in range(cut):
                 for d in range(line):
-                    slot = above[h].at[d * PAIR + x]
                     if d != zz:
-                        remote(zs.at[h, d], ru.at[h, d], zsend.at[h, d], urecv.at[h, d],
-                               mate).wait_send()
+                        up_copy(h, q, d, mate).wait_send()
                     if d <= zz and zz < line - 1:
-                        remote(slot, slot, asend.at[h, 0, d], arecv.at[h, d], mate).wait_send()
+                        line_hop(h, q, d, over, 0).wait_send()
                     if d >= zz and zz > 0:
-                        remote(slot, slot, asend.at[h, 1, d], arecv.at[h, d], mate).wait_send()
+                        line_hop(h, q, d, under, 1).wait_send()
+
+    by_line(drain)
+    for copy in stores:
+        copy.wait()
 
 
 def dense_on_device(right_sides, diag_inverse, off_diagonal, target_snode, target_block):
@@ -356,56 +439,69 @@
     outgoing = local * target_snode.shape[2]
     row_blocks = order // BR
     local_rows = local * row_blocks
-    chunk = local_rows * BR
     line = n // PAIR
     ymany = parts // PAIR
-    code = (target_snode * row_blocks + target_block).reshape(levels - 1, outgoing)
+    cut = local
+    piece = (local_rows * BR // cut, cols)
     bf, f32 = jnp.bfloat16, jnp.float32
     steps = levels - 1
     dma = pltpu.SemaphoreType.DMA
-    whole = pl.BlockSpec(memory_space=pltpu.VMEM)
+    vmem = pl.BlockSpec(memory_space=pltpu.VMEM)
+    smem = pl.BlockSpec(memory_space=pltpu.SMEM)
+    hbm = pl.BlockSpec(memory_space=pltpu.HBM)
     return pl.pallas_call(
         functools.partial(dense_kernel, n, parts),
         out_shape=jax.ShapeDtypeStruct(right_sides.shape, f32),
-        in_specs=[whole] * 4 + [pl.BlockSpec(memory_space=pltpu.SMEM)],
-        out_specs=whole,
+        in_specs=[hbm] * 3 + [vmem] * 2 + [smem] * 2,
+        out_specs=hbm,
         scratch_shapes=[
             pltpu.VMEM((levels, parts) + diag_inverse.shape[1:], f32),
             pltpu.VMEM((levels, local, 2, order, order), bf),
+            pltpu.VMEM(off_diagonal.shape, bf),
             pltpu.VMEM((steps, local, order, off_diagonal.shape[2]), bf),
             pltpu.VMEM(right_sides.shape, f32),
+            pltpu.VMEM(right_sides.shape, f32),
+            pltpu.VMEM(right_sides.shape, f32),
             pltpu.VMEM((outgoing * BR, cols), f32),
-            pltpu.VMEM((chunk, cols), f32),
-            pltpu.VMEM((steps, n, chunk, cols), bf),
-            pltpu.VMEM((steps, line, chunk, cols), bf),
-            pltpu.VMEM((steps, line, chunk, cols), bf),
-            pltpu.VMEM((steps, line, chunk, cols), bf),
-            pltpu.VMEM((steps, line, chunk, cols), bf),
+            pltpu.VMEM((local_rows * BR, cols), f32),
+            pltpu.VMEM((steps, cut, n) + piece, bf),
+            pltpu.VMEM((steps, cut, line) + piece, bf),
+            pltpu.VMEM((steps, cut, line) + piece, bf),
+            pltpu.VMEM((steps, cut, line) + piece, bf),
+            pltpu.VMEM((steps, cut, line) + piece, bf),
             [pltpu.VMEM((n, local_rows, BR, cols), bf)] * steps,
             pltpu.VMEM((outgoing * BR, cols), bf),
+            dma((3, levels)),
+            dma((levels,)),
             dma((levels, 2 * ymany)),
             dma((levels, 2 * ymany)),
-            dma((steps, line)),
-            dma((steps, line)),
-            dma((steps, line)),
-            dma((steps, line)),
-            dma((steps, line)),
-            dma((steps, 2, line)),
-            dma((steps, line)),
-            dma((steps, line)),
-            dma((steps, line)),
+            dma((steps, cut, line)),
+            dma((steps, cut, line)),
+            dma((steps, cut, line)),
+            dma((steps, cut, line)),
+            dma((steps, cut, line)),
+            dma((steps, 2, cut, line)),
+            dma((steps, cut, line)),
+            dma((steps, cut, line)),
+            dma((steps, cut, line)),
         ],
         compiler_params=pltpu.CompilerParams(
-            collective_id=0, has_side_effects=True, vmem_limit_bytes=48 * 1024 * 1024
+            collective_id=0, has_side_effects=True, vmem_limit_bytes=56 * 1024 * 1024
         ),
-    )(right_sides, diag_inverse, off_diagonal, code.reshape(steps, 1, outgoing), code)
+    )(right_sides, diag_inverse, off_diagonal, target_snode, target_block, target_snode,
+      target_block)
 
 
 def program(right_sides, diag_inverse, off_diagonal, target_snode, target_block):
     n, parts = lax.axis_size("snode"), lax.axis_size("rhs")
     capacity = 2 * right_sides.shape[1] * target_snode.shape[2] // n
     local_rows = right_sides.shape[1] * right_sides.shape[2] // BR
-    dense = capacity >= local_rows and n % PAIR == 0 and parts % PAIR == 0
+    dense = (
+        capacity >= local_rows
+        and n % PAIR == 0
+        and parts % PAIR == 0
+        and BR % right_sides.shape[1] == 0
+    )
     body = dense_on_device if dense else on_device
     return body(right_sides, diag_inverse, off_diagonal, target_snode, target_block)
 

time: 96.5 us -> 98.8 us (1.024)
  Pallas kernels: 90.8 us -> 96.6 us
  local copies, waits for them, and re-layouts: 4.76 us -> 2.06 us
    pallas_call x1, Pallas kernels: 90.8 us -> 96.6 us  [dense_on_device(): pl.pallas_call(functools.partial(dense_kernel, n, parts), out_shape=jax.S...]
    unnamed x7 -> x1, local copies, waits for them, and re-layouts: 4.6 us -> 2.06 us
where the time goes in v2:
time: 98.8 us; the launch traced here: 98.7 us
  Pallas kernels  96.6 us (98%)
  local copies, waits for them, and re-layouts  2.06 us (2%)
    pallas_call x1, Pallas kernels, dense_on_device(): pl.pallas_call(functools.partial(dense_kernel, n, parts), out_shape=jax.S...  96.6 us
    unnamed x1, local copies, waits for them, and re-layouts  2.06 us

profile of v2, /device:TPU:0, one launch (start us, length us, event | category | flops | bytes accessed | tf_op | source)
XLA Modules:
  0.0 98.7 jit_solution(629867238762111369)
XLA Ops:
  0.0 96.6 %shard_map.55 = f32[3,2,256,128]{3,2,1,0:T(8,128)} custom-call(f32[3,2,256,128]{3,2,1,0:T(8,128)} %rs_hbm.1, f32[3,2,64,256]{3,2,1,0:T(8,128)} %dg_ref.1, bf16[2,2,1024,256]{3,2,1,0:T(8,128)(2,1)} %od_hbm.1, s32[2,2,64]{2,1,0:T(2,128)} %snode_s.1, s32[2,2,64]{2,1,0:T(2,128)} %block_s.1, s32[2,2,64]{2,1,0:T(2,128)} %snode_s.1, s32[2,2,64]{2,1,0:T(2,128)} %block_s.1), custom_call_target="tpu_custom_call" | custom-call | tf_op jit(solution)/shard_map/pallas_call | solution.py:452
  96.6 2.1 %copy.7 = f32[3,2,256,128]{3,2,1,0:T(8,128)} copy(f32[3,2,256,128]{3,2,1,0:T(8,128)} %shard_map.55) | data formatting | bytes 1572864

commit v3 on v2

--- a/solution.py
+++ b/solution.py
@@ -135,9 +135,9 @@
 
 
 def dense_kernel(
-    n, parts, rs_hbm, dg_ref, od_hbm, snode_v, block_v, snode_s, block_s, out_hbm,
-    full, diag_t, od_ref, od_t, rs_ref, low, sol, upd, nat, part, rx, ru, rd, zs, above, picked,
-    lsend, osend, dsend, drecv, xsend, xrecv, zsend, urecv, wrecv, asend, arecv, bsend, brecv,
+    n, parts, rs_hbm, dg_ref, od_hbm, snode_v, block_v, snode_s, block_s, out_ref,
+    full, diag_t, od_ref, od_t, rs_ref, low, upd, nat, part, rx, rz, zs, above, picked,
+    lsend, dsend, drecv, xsend, xrecv, zsend, zrecv, asend, arecv, bsend, brecv,
 ):
     levels, local, order, cols = rs_ref.shape
     per_node = snode_v.shape[2]
@@ -153,8 +153,8 @@
     mine = lax.axis_index("rhs")
     yy, cc = mine // PAIR, mine % PAIR
     mate = {"snode": z * PAIR + (1 - x)}
-    over = {"snode": (z + 1) * PAIR + x}
-    under = {"snode": (z - 1) * PAIR + x}
+    away = [k for k in (2, 1) if k < line] + list(range(3, line))
+    peers = {k: {"snode": (z + k) % line * PAIR + x} for k in away}
     twin = {"rhs": yy * PAIR + (1 - cc)}
     sides = [(yy + k) % ymany for k in range(1, ymany)]
 
@@ -174,13 +174,8 @@
     for side in sides:
         greet({"rhs": side * PAIR + cc})
 
-    @pl.when(z > 0)
-    def _():
-        greet(under)
-
-    @pl.when(z < line - 1)
-    def _():
-        greet(over)
+    for k in away:
+        greet(peers[k])
 
     own_diag = [
         pltpu.make_async_copy(dg_ref.at[h], full.at[h, mine], lsend.at[0, h])
@@ -199,8 +194,7 @@
         if h < levels - 1:
             load_od[h].start()
 
-    ends = jnp.where(z > 0, 1, 0) + jnp.where(z < line - 1, 1, 0)
-    pl.semaphore_wait(barrier, 1 + ymany + ends)
+    pl.semaphore_wait(barrier, ymany + line)
 
     sent = []
 
@@ -238,7 +232,7 @@
         low[h, s] = mm3(high, low_part, residual)
 
     def backward(h, s, carried):
-        sol[h, s] = mm3(diag_t[h, s, 0], diag_t[h, s, 1], carried)
+        out_ref[h, s] = mm3(diag_t[h, s, 0], diag_t[h, s, 1], carried)
 
     def prepare(h):
         for s in range(local):
@@ -254,24 +248,13 @@
         code = snode_v[h] * row_blocks + block_v[h]
         return jnp.concatenate([code[s:s + 1] for s in range(local)], axis=1)
 
-    def by_line(body):
-        for zz in range(line):
-            @pl.when(z == zz)
-            def _(zz=zz):
-                body(zz)
-
-    def x_copy(h, q, d):
-        return remote(part.at[h, q, d * PAIR + (1 - x)], rx.at[h, q, d], xsend.at[h, q, d],
-                      xrecv.at[h, q, d], mate)
-
-    def up_copy(h, q, d, where):
-        return remote(zs.at[h, q, d], ru.at[h, q, d], zsend.at[h, q, d], urecv.at[h, q, d], where)
-
-    def down_copy(h, q, d, where):
-        return remote(zs.at[h, q, d], rd.at[h, q, d], zsend.at[h, q, d], wrecv.at[h, q, d], where)
-
-    def far_first(zz):
-        return sorted(range(line), key=lambda d: -abs(d - zz))
+    def x_copy(h, q, k):
+        d = (z + k) % line
+        return remote(part.at[h, q, d * PAIR + (1 - x)], rx.at[h, q, k], xsend.at[h, q, k],
+                      xrecv.at[h, q, k], mate)
+
+    def z_copy(h, q, k):
+        return remote(zs.at[h, q, k], rz.at[h, q, k], zsend.at[h, q, k], zrecv.at[h, q, k], peers[k])
 
     first = start_gather(0)
     tables = []
@@ -299,11 +282,8 @@
                         summed[d * local_rows:(d + 1) * local_rows]
                     )
 
-            def send_x(zz, q=q, h=h):
-                for d in far_first(zz):
-                    x_copy(h, q, d).start()
-
-            by_line(send_x)
+            for k in away + [0]:
+                x_copy(h, q, k).start()
 
         if h == 0:
             prepare(0)
@@ -313,88 +293,65 @@
                 finish_gather(later, *gather[later])
                 prepare(later)
 
-        for q in range(cut):
-            def reduce(zz, q=q, h=h):
-                for d in far_first(zz):
-                    x_copy(h, q, d).wait_recv()
-                    total = (part[h, q, d * PAIR + x].astype(jnp.float32)
-                             + rx[h, q, d].astype(jnp.float32))
-                    if d >= zz and zz > 0:
-                        up_copy(h, q, d, under).wait_recv()
-                        total = total + ru[h, q, d].astype(jnp.float32)
-                    if d <= zz and zz < line - 1:
-                        down_copy(h, q, d, over).wait_recv()
-                        total = total + rd[h, q, d].astype(jnp.float32)
-                    if d != zz:
-                        zs[h, q, d] = total.astype(jnp.bfloat16)
-                    if d > zz:
-                        up_copy(h, q, d, over).start()
-                    elif d < zz:
-                        down_copy(h, q, d, under).start()
-                    else:
-                        for r in range(width):
-                            nat[pl.ds(q * width + r, local_rows, stride=BR), :] = (
-                                total[r * local_rows:(r + 1) * local_rows]
-                            )
-
-            by_line(reduce)
-            if h == 0 and q == 0:
-                finish_gather(1, *gather[1])
+        def paired(q, k):
+            x_copy(h, q, k).wait_recv()
+            own = part[h, q, (z + k) % line * PAIR + x]
+            return own.astype(jnp.float32) + rx[h, q, k].astype(jnp.float32)
+
+        for q in range(cut):
+            for k in away:
+                zs[h, q, k] = paired(q, k).astype(jnp.bfloat16)
+                z_copy(h, q, k).start()
+        if h == 0:
+            finish_gather(1, *gather[1])
+        for q in range(cut):
+            total = paired(q, 0)
+            for k in away:
+                z_copy(h, q, k).wait_recv()
+                total = total + rz[h, q, k].astype(jnp.float32)
+            for r in range(width):
+                nat[pl.ds(q * width + r, local_rows, stride=BR), :] = (
+                    total[r * local_rows:(r + 1) * local_rows]
+                )
         load_rs[h + 1].wait()
         for s in range(local):
             forward(h + 1, s, rs_ref[h + 1, s] - nat[pl.ds(s * order, order), :])
 
-    stores = []
-
-    def store(h):
-        copy = pltpu.make_async_copy(sol.at[h], out_hbm.at[h], osend.at[h])
-        copy.start()
-        stores.append(copy)
-
-    def hop(h, q, s, where, s_sem, r_sem, col):
-        slot = above[h].at[s * PAIR + col, pl.ds(q * row_blocks, row_blocks)]
+    def hop(h, q, source, where, s_sem, r_sem, col):
+        slot = above[h].at[source * PAIR + col, pl.ds(q * row_blocks, row_blocks)]
         return remote(slot, slot, s_sem, r_sem, where)
 
-    def line_hop(h, q, s, where, way):
-        return hop(h, q, s, where, asend.at[h, way, q, s], arecv.at[h, q, s], x)
-
-    def mate_hop(h, q, s, col):
-        return hop(h, q, s, mate, bsend.at[h, q, s], brecv.at[h, q, s], col)
-
-    def pass_on(h, q, s, zz):
-        if s <= zz and zz < line - 1:
-            line_hop(h, q, s, over, 0).start()
-        if s >= zz and zz > 0:
-            line_hop(h, q, s, under, 1).start()
-        mate_hop(h, q, s, x).start()
+    def line_hop(h, q, k, source):
+        return hop(h, q, source, peers[k], asend.at[h, q, k], arecv.at[h, q, k], x)
+
+    def mate_hop(h, q, k, col):
+        source = (z + line - k) % line
+        return hop(h, q, source, mate, bsend.at[h, q, k], brecv.at[h, q, k], col)
 
     def publish(h, q):
         above[h][me, q * row_blocks:(q + 1) * row_blocks] = (
-            sol[h + 1, q].reshape(row_blocks, BR, cols).astype(jnp.bfloat16)
-        )
-        by_line(lambda zz: pass_on(h, q, zz, zz))
+            out_ref[h + 1, q].reshape(row_blocks, BR, cols).astype(jnp.bfloat16)
+        )
+        for k in away:
+            line_hop(h, q, k, z).start()
+        mate_hop(h, q, 0, x).start()
 
     for s in range(local):
         backward(levels - 1, s, low[levels - 1, s])
         publish(levels - 2, s)
-    store(levels - 1)
 
     for h in range(levels - 2, -1, -1):
         if h > 0:
             turn(h)
             prepare(h)
 
-        def spread(zz, h=h):
-            for s in sorted(range(line), key=lambda s: abs(s - zz)):
-                for q in range(cut):
-                    if s != zz:
-                        line_hop(h, q, s, over, 0).wait_recv()
-                        pass_on(h, q, s, zz)
-
-        by_line(spread)
-        for s in range(line):
-            for q in range(cut):
-                mate_hop(h, q, s, 1 - x).wait_recv()
+        for q in range(cut):
+            for k in away:
+                line_hop(h, q, k, (z + line - k) % line).wait_recv()
+                mate_hop(h, q, k, x).start()
+        for q in range(cut):
+            for k in range(line):
+                mate_hop(h, q, k, 1 - x).wait_recv()
         for s in range(local):
             for k in range(per_node):
                 picked[pl.ds((s * per_node + k) * BR, BR), :] = above[h][
@@ -407,30 +364,17 @@
             backward(h, s, carried)
             if h > 0:
                 publish(h - 1, s)
-        store(h)
 
     for copy in sent:
         copy.wait_send()
     for h in range(levels - 1):
         for q in range(cut):
-            for d in range(line):
-                x_copy(h, q, d).wait_send()
-                mate_hop(h, q, d, x).wait_send()
-
-    def drain(zz):
-        for h in range(levels - 1):
-            for q in range(cut):
-                for d in range(line):
-                    if d != zz:
-                        up_copy(h, q, d, mate).wait_send()
-                    if d <= zz and zz < line - 1:
-                        line_hop(h, q, d, over, 0).wait_send()
-                    if d >= zz and zz > 0:
-                        line_hop(h, q, d, under, 1).wait_send()
-
-    by_line(drain)
-    for copy in stores:
-        copy.wait()
+            for k in range(line):
+                x_copy(h, q, k).wait_send()
+                mate_hop(h, q, k, x).wait_send()
+            for k in away:
+                z_copy(h, q, k).wait_send()
+                line_hop(h, q, k, z).wait_send()
 
 
 def dense_on_device(right_sides, diag_inverse, off_diagonal, target_snode, target_block):
@@ -453,13 +397,12 @@
         functools.partial(dense_kernel, n, parts),
         out_shape=jax.ShapeDtypeStruct(right_sides.shape, f32),
         in_specs=[hbm] * 3 + [vmem] * 2 + [smem] * 2,
-        out_specs=hbm,
+        out_specs=vmem,
         scratch_shapes=[
             pltpu.VMEM((levels, parts) + diag_inverse.shape[1:], f32),
             pltpu.VMEM((levels, local, 2, order, order), bf),
             pltpu.VMEM(off_diagonal.shape, bf),
             pltpu.VMEM((steps, local, order, off_diagonal.shape[2]), bf),
-            pltpu.VMEM(right_sides.shape, f32),
             pltpu.VMEM(right_sides.shape, f32),
             pltpu.VMEM(right_sides.shape, f32),
             pltpu.VMEM((outgoing * BR, cols), f32),
@@ -468,11 +411,9 @@
             pltpu.VMEM((steps, cut, line) + piece, bf),
             pltpu.VMEM((steps, cut, line) + piece, bf),
             pltpu.VMEM((steps, cut, line) + piece, bf),
-            pltpu.VMEM((steps, cut, line) + piece, bf),
             [pltpu.VMEM((n, local_rows, BR, cols), bf)] * steps,
             pltpu.VMEM((outgoing * BR, cols), bf),
             dma((3, levels)),
-            dma((levels,)),
             dma((levels, 2 * ymany)),
             dma((levels, 2 * ymany)),
             dma((steps, cut, line)),
@@ -480,7 +421,6 @@
             dma((steps, cut, line)),
             dma((steps, cut, line)),
             dma((steps, cut, line)),
-            dma((steps, 2, cut, line)),
             dma((steps, cut, line)),
             dma((steps, cut, line)),
             dma((steps, cut, line)),

time: 98.8 us -> 87.6 us (0.89)
  Pallas kernels: 96.6 us -> 85.1 us
    pallas_call x1, Pallas kernels: 96.6 us -> 85.1 us  [dense_on_device(): pl.pallas_call(functools.partial(dense_kernel, n, parts), out_shape=jax.S...]
where the time goes in v3:
time: 87.6 us; the launch traced here: 87.2 us
  Pallas kernels  85.1 us (97%)
  local copies, waits for them, and re-layouts  2.06 us (2%)
    pallas_call x1, Pallas kernels, dense_on_device(): pl.pallas_call(functools.partial(dense_kernel, n, parts), out_shape=jax.S...  85.1 us
    unnamed x1, local copies, waits for them, and re-layouts  2.06 us

profile of v3, /device:TPU:0, one launch (start us, length us, event | category | flops | bytes accessed | tf_op | source)
XLA Modules:
  0.0 87.2 jit_solution(14876063047914452791)
XLA Ops:
  0.0 85.1 %shard_map.55 = f32[3,2,256,128]{3,2,1,0:T(8,128)} custom-call(f32[3,2,256,128]{3,2,1,0:T(8,128)} %rs_hbm.1, f32[3,2,64,256]{3,2,1,0:T(8,128)} %dg_ref.1, bf16[2,2,1024,256]{3,2,1,0:T(8,128)(2,1)} %od_hbm.1, s32[2,2,64]{2,1,0:T(2,128)} %snode_s.1, s32[2,2,64]{2,1,0:T(2,128)} %block_s.1, s32[2,2,64]{2,1,0:T(2,128)} %snode_s.1, s32[2,2,64]{2,1,0:T(2,128)} %block_s.1), custom_call_target="tpu_custom_call" | custom-call | tf_op jit(solution)/shard_map/pallas_call | solution.py:396
  85.1 2.1 %copy.7 = f32[3,2,256,128]{3,2,1,0:T(8,128)} copy(f32[3,2,256,128]{3,2,1,0:T(8,128)} %shard_map.55) | data formatting | bytes 1572864

commit v4 on v3

--- a/solution.py
+++ b/solution.py
@@ -209,7 +209,7 @@
         own.start()
         return near, own
 
-    def finish_gather(h, near, own):
+    def finish_gather(h, near, own, meanwhile=None):
         hops = []
         for k, copy in enumerate(near):
             copy.wait_recv()
@@ -218,6 +218,8 @@
                          drecv.at[h, ymany + 1 + k], twin)
             hop.start()
             hops.append(hop)
+        if meanwhile is not None:
+            meanwhile()
         own.wait_recv()
         own_diag[h].wait()
         for hop in hops:
@@ -261,14 +263,21 @@
     rows = lax.broadcasted_iota(jnp.int32, (n * local_rows, outgoing), 0)
     for h in range(levels - 1):
         tables.append(jnp.where(rows == codes(h), 1.0, 0.0).astype(jnp.bfloat16))
-    finish_gather(0, *first)
+    load_od[0].wait()
+    turn(0)
+
+    def turn_rest():
+        for h in range(1, levels - 1):
+            load_od[h].wait()
+            turn(h)
+
+    finish_gather(0, *first, meanwhile=turn_rest)
     gather = [None] + [start_gather(h) for h in range(1, levels)]
     load_rs[0].wait()
     for s in range(local):
         forward(0, s, rs_ref[0, s])
 
     for h in range(levels - 1):
-        load_od[h].wait()
         for s in range(local):
             upd[pl.ds(s * per_node * BR, per_node * BR), :] = mm(
                 od_ref[h, s], low[h, s].astype(jnp.bfloat16)
@@ -285,14 +294,6 @@
             for k in away + [0]:
                 x_copy(h, q, k).start()
 
-        if h == 0:
-            prepare(0)
-            turn(0)
-        if h == levels - 2:
-            for later in range(max(h + 1, 2), levels):
-                finish_gather(later, *gather[later])
-                prepare(later)
-
         def paired(q, k):
             x_copy(h, q, k).wait_recv()
             own = part[h, q, (z + k) % line * PAIR + x]
@@ -302,8 +303,10 @@
             for k in away:
                 zs[h, q, k] = paired(q, k).astype(jnp.bfloat16)
                 z_copy(h, q, k).start()
-        if h == 0:
-            finish_gather(1, *gather[1])
+        prepare(h)
+        finish_gather(h + 1, *gather[h + 1])
+        if h == levels - 2:
+            prepare(levels - 1)
         for q in range(cut):
             total = paired(q, 0)
             for k in away:
@@ -318,7 +321,9 @@
             forward(h + 1, s, rs_ref[h + 1, s] - nat[pl.ds(s * order, order), :])
 
     def hop(h, q, source, where, s_sem, r_sem, col):
-        slot = above[h].at[source * PAIR + col, pl.ds(q * row_blocks, row_blocks)]
+        slot = above[h].at[
+            pl.ds(((source * PAIR + col) * local + q) * row_blocks, row_blocks)
+        ]
         return remote(slot, slot, s_sem, r_sem, where)
 
     def line_hop(h, q, k, source):
@@ -329,22 +334,18 @@
         return hop(h, q, source, mate, bsend.at[h, q, k], brecv.at[h, q, k], col)
 
     def publish(h, q):
-        above[h][me, q * row_blocks:(q + 1) * row_blocks] = (
+        above[h][pl.ds((me * local + q) * row_blocks, row_blocks)] = (
             out_ref[h + 1, q].reshape(row_blocks, BR, cols).astype(jnp.bfloat16)
         )
+        mate_hop(h, q, 0, x).start()
         for k in away:
             line_hop(h, q, k, z).start()
-        mate_hop(h, q, 0, x).start()
 
     for s in range(local):
         backward(levels - 1, s, low[levels - 1, s])
         publish(levels - 2, s)
 
     for h in range(levels - 2, -1, -1):
-        if h > 0:
-            turn(h)
-            prepare(h)
-
         for q in range(cut):
             for k in away:
                 line_hop(h, q, k, (z + line - k) % line).wait_recv()
@@ -355,8 +356,7 @@
         for s in range(local):
             for k in range(per_node):
                 picked[pl.ds((s * per_node + k) * BR, BR), :] = above[h][
-                    snode_s[h, s, k] // local,
-                    snode_s[h, s, k] % local * row_blocks + block_s[h, s, k],
+                    snode_s[h, s, k] * row_blocks + block_s[h, s, k]
                 ]
             carried = low[h, s] - mm(
                 od_t[h, s], picked[pl.ds(s * per_node * BR, per_node * BR), :]
@@ -411,7 +411,7 @@
             pltpu.VMEM((steps, cut, line) + piece, bf),
             pltpu.VMEM((steps, cut, line) + piece, bf),
             pltpu.VMEM((steps, cut, line) + piece, bf),
-            [pltpu.VMEM((n, local_rows, BR, cols), bf)] * steps,
+            [pltpu.VMEM((n * local_rows, BR, cols), bf)] * steps,
             pltpu.VMEM((outgoing * BR, cols), bf),
             dma((3, levels)),
             dma((levels, 2 * ymany)),
@@ -426,7 +426,7 @@
             dma((steps, cut, line)),
         ],
         compiler_params=pltpu.CompilerParams(
-            collective_id=0, has_side_effects=True, vmem_limit_bytes=56 * 1024 * 1024
+            collective_id=0, has_side_effects=True, vmem_limit_bytes=40 * 1024 * 1024
         ),
     )(right_sides, diag_inverse, off_diagonal, target_snode, target_block, target_snode,
       target_block)

time: 87.6 us -> 90.1 us (1.029)
  local copies, waits for them, and re-layouts: 2.06 us -> 5.96 us
  Pallas kernels: 85.1 us -> 83.9 us
    unnamed x1 -> x11, local copies, waits for them, and re-layouts: 2.06 us -> 5.96 us
    pallas_call x1, Pallas kernels: 85.1 us -> 83.9 us  [dense_on_device(): pl.pallas_call(functools.partial(dense_kernel, n, parts), out_shape=jax.S...]
where the time goes in v4:
time: 90.1 us; the launch traced here: 89.8 us
  Pallas kernels  83.9 us (93%)
  local copies, waits for them, and re-layouts  5.96 us (7%)
    pallas_call x1, Pallas kernels, dense_on_device(): pl.pallas_call(functools.partial(dense_kernel, n, parts), out_shape=jax.S...  83.9 us
    unnamed x11, local copies, waits for them, and re-layouts  5.96 us

profile of v4, /device:TPU:0, one launch (start us, length us, event | category | flops | bytes accessed | tf_op | source)
XLA Modules:
  0.0 89.8 jit_solution(4531270636595034877)
XLA Ops:
  0.0 0.0 copy-start
  0.0 1.6 %copy-done = bf16[2,2,1024,256]{3,2,1,0:T(8,128)(2,1)S(1)} copy-done((bf16[2,2,1024,256]{3,2,1,0:T(8,128)(2,1)S(1)}, bf16[2,2,1024,256]{3,2,1,0:T(8,128)(2,1)}, u32[]{:S(2)}) %copy-start) | copy-done | bytes 2097176
  1.6 0.0 copy-start.1
  1.6 1.1 %copy-done.1 = f32[3,2,256,128]{3,2,1,0:T(8,128)S(1)} copy-done((f32[3,2,256,128]{3,2,1,0:T(8,128)S(1)}, f32[3,2,256,128]{3,2,1,0:T(8,128)}, u32[]{:S(2)}) %copy-start.1) | copy-done | bytes 786456
  2.7 0.0 copy-start.2
  2.7 1.0 %copy-done.2 = f32[3,2,64,256]{3,2,1,0:T(8,128)S(1)} copy-done((f32[3,2,64,256]{3,2,1,0:T(8,128)S(1)}, f32[3,2,64,256]{3,2,1,0:T(8,128)}, u32[]{:S(2)}) %copy-start.2) | copy-done | bytes 393240
  3.7 0.0 copy-start.3
  3.7 0.7 copy-done.3
  4.4 0.0 copy-start.4
  4.4 0.7 copy-done.4
  5.1 83.9 %shard_map.55 = f32[3,2,256,128]{3,2,1,0:T(8,128)S(1)} custom-call(f32[3,2,256,128]{3,2,1,0:T(8,128)S(1)} %copy-done.1, f32[3,2,64,256]{3,2,1,0:T(8,128)S(1)} %copy-done.2, bf16[2,2,1024,256]{3,2,1,0:T(8,128)(2,1)S(1)} %copy-done, s32[2,2,64]{2,1,0:T(2,128)S(1)} %copy-done.3, s32[2,2,64]{2,1,0:T(2,128)S(1)} %copy-done.4, s32[2,2,64]{2,1,0:T(2,128)S(1)} %copy-done.3, ...), custom_call_target="tpu_custom_call" | custom-call | tf_op jit(solution)/shard_map/pallas_call | solution.py:396
  89.0 0.9 copy.7
Async XLA Ops:
  0.0 1.6 %copy-start = (bf16[2,2,1024,256]{3,2,1,0:T(8,128)(2,1)S(1)}, bf16[2,2,1024,256]{3,2,1,0:T(8,128)(2,1)}, u32[]{:S(2)}) copy-start(bf16[2,2,1024,256]{3,2,1,0:T(8,128)(2,1)} %od_hbm.1) | copy-start | bytes 6291460
  1.6 1.1 %copy-start.1 = (f32[3,2,256,128]{3,2,1,0:T(8,128)S(1)}, f32[3,2,256,128]{3,2,1,0:T(8,128)}, u32[]{:S(2)}) copy-start(f32[3,2,256,128]{3,2,1,0:T(8,128)} %rs_hbm.1) | copy-start | bytes 2359300
  2.7 1.0 %copy-start.2 = (f32[3,2,64,256]{3,2,1,0:T(8,128)S(1)}, f32[3,2,64,256]{3,2,1,0:T(8,128)}, u32[]{:S(2)}) copy-start(f32[3,2,64,256]{3,2,1,0:T(8,128)} %dg_ref.1) | copy-start | bytes 1179652
  3.7 0.7 copy-start.3
  4.4 0.7 copy-start.4

commit v5 on v4

--- a/solution.py
+++ b/solution.py
@@ -137,7 +137,7 @@
 def dense_kernel(
     n, parts, rs_hbm, dg_ref, od_hbm, snode_v, block_v, snode_s, block_s, out_ref,
     full, diag_t, od_ref, od_t, rs_ref, low, upd, nat, part, rx, rz, zs, above, picked,
-    lsend, dsend, drecv, xsend, xrecv, zsend, zrecv, asend, arecv, bsend, brecv,
+    lsend, dsend, drecv, xsend, xrecv, zsend, zrecv, asend, arecv, bsend, brecv, token,
 ):
     levels, local, order, cols = rs_ref.shape
     per_node = snode_v.shape[2]
@@ -291,6 +291,11 @@
                         summed[d * local_rows:(d + 1) * local_rows]
                     )
 
+            if h == 0 and q == 0:
+                @pl.when(cc == 0)
+                def _():
+                    pl.semaphore_wait(token, 1)
+
             for k in away + [0]:
                 x_copy(h, q, k).start()
 
@@ -303,6 +308,15 @@
             for k in away:
                 zs[h, q, k] = paired(q, k).astype(jnp.bfloat16)
                 z_copy(h, q, k).start()
+        if h == 0:
+            for q in range(cut):
+                for k in range(line):
+                    x_copy(h, q, k).wait_send()
+
+            @pl.when(cc == 1)
+            def _():
+                pl.semaphore_signal(token, inc=1, device_id=twin, device_id_type=MESH)
+
         prepare(h)
         finish_gather(h + 1, *gather[h + 1])
         if h == levels - 2:
@@ -370,7 +384,8 @@
     for h in range(levels - 1):
         for q in range(cut):
             for k in range(line):
-                x_copy(h, q, k).wait_send()
+                if h > 0:
+                    x_copy(h, q, k).wait_send()
                 mate_hop(h, q, k, x).wait_send()
             for k in away:
                 z_copy(h, q, k).wait_send()
@@ -424,9 +439,10 @@
             dma((steps, cut, line)),
             dma((steps, cut, line)),
             dma((steps, cut, line)),
+            pltpu.SemaphoreType.REGULAR,
         ],
         compiler_params=pltpu.CompilerParams(
-            collective_id=0, has_side_effects=True, vmem_limit_bytes=40 * 1024 * 1024
+            collective_id=0, has_side_effects=True, vmem_limit_bytes=56 * 1024 * 1024
         ),
     )(right_sides, diag_inverse, off_diagonal, target_snode, target_block, target_snode,
       target_block)

time: 90.1 us -> 83.3 us (0.925)
  local copies, waits for them, and re-layouts: 5.96 us -> 2.06 us
  Pallas kernels: 83.9 us -> 81.1 us
    unnamed x11 -> x1, local copies, waits for them, and re-layouts: 5.96 us -> 2.06 us
    pallas_call x1, Pallas kernels: 83.9 us -> 81.1 us  [dense_on_device(): pl.pallas_call(functools.partial(dense_kernel, n, parts), out_shape=jax.S...]
where the time goes in v5:
time: 83.3 us; the launch traced here: 83.1 us
  Pallas kernels  81.1 us (97%)
  local copies, waits for them, and re-layouts  2.06 us (2%)
    pallas_call x1, Pallas kernels, dense_on_device(): pl.pallas_call(functools.partial(dense_kernel, n, parts), out_shape=jax.S...  81.1 us
    unnamed x1, local copies, waits for them, and re-layouts  2.06 us

profile of v5, /device:TPU:0, one launch (start us, length us, event | category | flops | bytes accessed | tf_op | source)
XLA Modules:
  0.0 83.1 jit_solution(8090349626442969554)
XLA Ops:
  0.0 81.1 %shard_map.55 = f32[3,2,256,128]{3,2,1,0:T(8,128)} custom-call(f32[3,2,256,128]{3,2,1,0:T(8,128)} %rs_hbm.1, f32[3,2,64,256]{3,2,1,0:T(8,128)} %dg_ref.1, bf16[2,2,1024,256]{3,2,1,0:T(8,128)(2,1)} %od_hbm.1, s32[2,2,64]{2,1,0:T(2,128)} %snode_s.1, s32[2,2,64]{2,1,0:T(2,128)} %block_s.1, s32[2,2,64]{2,1,0:T(2,128)} %snode_s.1, s32[2,2,64]{2,1,0:T(2,128)} %block_s.1), custom_call_target="tpu_custom_call" | custom-call | tf_op jit(solution)/shard_map/pallas_call | solution.py:411
  81.1 2.1 %copy.7 = f32[3,2,256,128]{3,2,1,0:T(8,128)} copy(f32[3,2,256,128]{3,2,1,0:T(8,128)} %shard_map.55) | data formatting | bytes 1572864

commit v6 on v5

--- a/solution.py
+++ b/solution.py
@@ -153,8 +153,24 @@
     mine = lax.axis_index("rhs")
     yy, cc = mine // PAIR, mine % PAIR
     mate = {"snode": z * PAIR + (1 - x)}
-    away = [k for k in (2, 1) if k < line] + list(range(3, line))
-    peers = {k: {"snode": (z + k) % line * PAIR + x} for k in away}
+    bits = [1 << i for i in range(line.bit_length() - 1)]
+
+    def flip(f):
+        other = z
+        for b in bits:
+            if f & b:
+                other = other + b - 2 * b * ((z // b) % 2)
+        return other
+
+    def lowest(f):
+        return f & -f if f else line
+
+    def feeders(f):
+        return [f | b for b in bits if b < lowest(f)]
+
+    peers = {b: {"snode": flip(b) * PAIR + x} for b in bits}
+    inward = sorted(range(1, line), key=lambda f: (lowest(f), -f))
+    outward = sorted(range(1, line), key=lambda f: (-lowest(f), f))
     twin = {"rhs": yy * PAIR + (1 - cc)}
     sides = [(yy + k) % ymany for k in range(1, ymany)]
 
@@ -174,8 +190,8 @@
     for side in sides:
         greet({"rhs": side * PAIR + cc})
 
-    for k in away:
-        greet(peers[k])
+    for b in bits:
+        greet(peers[b])
 
     own_diag = [
         pltpu.make_async_copy(dg_ref.at[h], full.at[h, mine], lsend.at[0, h])
@@ -194,7 +210,7 @@
         if h < levels - 1:
             load_od[h].start()
 
-    pl.semaphore_wait(barrier, ymany + line)
+    pl.semaphore_wait(barrier, ymany + 1 + len(bits))
 
     sent = []
 
@@ -251,12 +267,12 @@
         return jnp.concatenate([code[s:s + 1] for s in range(local)], axis=1)
 
     def x_copy(h, q, k):
-        d = (z + k) % line
-        return remote(part.at[h, q, d * PAIR + (1 - x)], rx.at[h, q, k], xsend.at[h, q, k],
+        return remote(part.at[h, q, flip(k) * PAIR + (1 - x)], rx.at[h, q, k], xsend.at[h, q, k],
                       xrecv.at[h, q, k], mate)
 
     def z_copy(h, q, k):
-        return remote(zs.at[h, q, k], rz.at[h, q, k], zsend.at[h, q, k], zrecv.at[h, q, k], peers[k])
+        return remote(zs.at[h, q, k], rz.at[h, q, k], zsend.at[h, q, k], zrecv.at[h, q, k],
+                      peers[lowest(k)])
 
     first = start_gather(0)
     tables = []
@@ -296,16 +312,20 @@
                 def _():
                     pl.semaphore_wait(token, 1)
 
-            for k in away + [0]:
+            for k in inward + [0]:
                 x_copy(h, q, k).start()
 
         def paired(q, k):
             x_copy(h, q, k).wait_recv()
-            own = part[h, q, (z + k) % line * PAIR + x]
-            return own.astype(jnp.float32) + rx[h, q, k].astype(jnp.float32)
+            own = part[h, q, flip(k) * PAIR + x]
+            total = own.astype(jnp.float32) + rx[h, q, k].astype(jnp.float32)
+            for f in feeders(k):
+                z_copy(h, q, f).wait_recv()
+                total = total + rz[h, q, f].astype(jnp.float32)
+            return total
 
         for q in range(cut):
-            for k in away:
+            for k in inward:
                 zs[h, q, k] = paired(q, k).astype(jnp.bfloat16)
                 z_copy(h, q, k).start()
         if h == 0:
@@ -323,9 +343,6 @@
             prepare(levels - 1)
         for q in range(cut):
             total = paired(q, 0)
-            for k in away:
-                z_copy(h, q, k).wait_recv()
-                total = total + rz[h, q, k].astype(jnp.float32)
             for r in range(width):
                 nat[pl.ds(q * width + r, local_rows, stride=BR), :] = (
                     total[r * local_rows:(r + 1) * local_rows]
@@ -341,28 +358,29 @@
         return remote(slot, slot, s_sem, r_sem, where)
 
     def line_hop(h, q, k, source):
-        return hop(h, q, source, peers[k], asend.at[h, q, k], arecv.at[h, q, k], x)
+        return hop(h, q, source, peers[lowest(k)], asend.at[h, q, k], arecv.at[h, q, k], x)
 
     def mate_hop(h, q, k, col):
-        source = (z + line - k) % line
-        return hop(h, q, source, mate, bsend.at[h, q, k], brecv.at[h, q, k], col)
+        return hop(h, q, flip(k), mate, bsend.at[h, q, k], brecv.at[h, q, k], col)
 
     def publish(h, q):
         above[h][pl.ds((me * local + q) * row_blocks, row_blocks)] = (
             out_ref[h + 1, q].reshape(row_blocks, BR, cols).astype(jnp.bfloat16)
         )
         mate_hop(h, q, 0, x).start()
-        for k in away:
-            line_hop(h, q, k, z).start()
+        for b in reversed(bits):
+            line_hop(h, q, b, z).start()
 
     for s in range(local):
         backward(levels - 1, s, low[levels - 1, s])
         publish(levels - 2, s)
 
     for h in range(levels - 2, -1, -1):
-        for q in range(cut):
-            for k in away:
-                line_hop(h, q, k, (z + line - k) % line).wait_recv()
+        for k in outward:
+            for q in range(cut):
+                line_hop(h, q, k, flip(k)).wait_recv()
+                for f in feeders(k):
+                    line_hop(h, q, f, flip(k)).start()
                 mate_hop(h, q, k, x).start()
         for q in range(cut):
             for k in range(line):
@@ -387,7 +405,7 @@
                 if h > 0:
                     x_copy(h, q, k).wait_send()
                 mate_hop(h, q, k, x).wait_send()
-            for k in away:
+            for k in inward:
                 z_copy(h, q, k).wait_send()
                 line_hop(h, q, k, z).wait_send()
 
@@ -455,6 +473,7 @@
     dense = (
         capacity >= local_rows
         and n % PAIR == 0
+        and (n // PAIR) & (n // PAIR - 1) == 0
         and parts % PAIR == 0
         and BR % right_sides.shape[1] == 0
     )

time: 83.3 us -> 86 us (1.032)
  Pallas kernels: 81.1 us -> 83.8 us
    pallas_call x1, Pallas kernels: 81.1 us -> 83.8 us  [dense_on_device(): pl.pallas_call(functools.partial(dense_kernel, n, parts), out_shape=jax.S...]
where the time goes in v6:
time: 86 us; the launch traced here: 85.8 us
  Pallas kernels  83.8 us (97%)
  local copies, waits for them, and re-layouts  2.06 us (2%)
    pallas_call x1, Pallas kernels, dense_on_device(): pl.pallas_call(functools.partial(dense_kernel, n, parts), out_shape=jax.S...  83.8 us
    unnamed x1, local copies, waits for them, and re-layouts  2.06 us

profile of v6, /device:TPU:0, one launch (start us, length us, event | category | flops | bytes accessed | tf_op | source)
XLA Modules:
  0.0 85.8 jit_solution(14832027755798803590)
XLA Ops:
  0.0 83.8 %shard_map.55 = f32[3,2,256,128]{3,2,1,0:T(8,128)} custom-call(f32[3,2,256,128]{3,2,1,0:T(8,128)} %rs_hbm.1, f32[3,2,64,256]{3,2,1,0:T(8,128)} %dg_ref.1, bf16[2,2,1024,256]{3,2,1,0:T(8,128)(2,1)} %od_hbm.1, s32[2,2,64]{2,1,0:T(2,128)} %snode_s.1, s32[2,2,64]{2,1,0:T(2,128)} %block_s.1, s32[2,2,64]{2,1,0:T(2,128)} %snode_s.1, s32[2,2,64]{2,1,0:T(2,128)} %block_s.1), custom_call_target="tpu_custom_call" | custom-call | tf_op jit(solution)/shard_map/pallas_call | solution.py:429
  83.8 2.1 %copy.7 = f32[3,2,256,128]{3,2,1,0:T(8,128)} copy(f32[3,2,256,128]{3,2,1,0:T(8,128)} %shard_map.55) | data formatting | bytes 1572864

commit v7 on v5

--- a/solution.py
+++ b/solution.py
@@ -135,7 +135,7 @@
 
 
 def dense_kernel(
-    n, parts, rs_hbm, dg_ref, od_hbm, snode_v, block_v, snode_s, block_s, out_ref,
+    n, parts, rs_hbm, dg_ref, od_hbm, snode_v, block_v, snode_s, block_s, outs,
     full, diag_t, od_ref, od_t, rs_ref, low, upd, nat, part, rx, rz, zs, above, picked,
     lsend, dsend, drecv, xsend, xrecv, zsend, zrecv, asend, arecv, bsend, brecv, token,
 ):
@@ -234,7 +234,7 @@
         low[h, s] = mm3(high, low_part, residual)
 
     def backward(h, s, carried):
-        out_ref[h, s] = mm3(diag_t[h, s, 0], diag_t[h, s, 1], carried)
+        outs[h][s] = mm3(diag_t[h, s, 0], diag_t[h, s, 1], carried)
 
     def prepare(h):
         for s in range(local):
@@ -317,7 +317,8 @@
             def _():
                 pl.semaphore_signal(token, inc=1, device_id=twin, device_id_type=MESH)
 
-        prepare(h)
+        if h == 0:
+            prepare(0)
         finish_gather(h + 1, *gather[h + 1])
         if h == levels - 2:
             prepare(levels - 1)
@@ -349,7 +350,7 @@
 
     def publish(h, q):
         above[h][pl.ds((me * local + q) * row_blocks, row_blocks)] = (
-            out_ref[h + 1, q].reshape(row_blocks, BR, cols).astype(jnp.bfloat16)
+            outs[h + 1][q].reshape(row_blocks, BR, cols).astype(jnp.bfloat16)
         )
         mate_hop(h, q, 0, x).start()
         for k in away:
@@ -360,6 +361,8 @@
         publish(levels - 2, s)
 
     for h in range(levels - 2, -1, -1):
+        if h > 0:
+            prepare(h)
         for q in range(cut):
             for k in away:
                 line_hop(h, q, k, (z + line - k) % line).wait_recv()
@@ -408,11 +411,11 @@
     vmem = pl.BlockSpec(memory_space=pltpu.VMEM)
     smem = pl.BlockSpec(memory_space=pltpu.SMEM)
     hbm = pl.BlockSpec(memory_space=pltpu.HBM)
-    return pl.pallas_call(
+    answers = pl.pallas_call(
         functools.partial(dense_kernel, n, parts),
-        out_shape=jax.ShapeDtypeStruct(right_sides.shape, f32),
+        out_shape=[[jax.ShapeDtypeStruct(right_sides.shape[1:], f32)] * levels],
         in_specs=[hbm] * 3 + [vmem] * 2 + [smem] * 2,
-        out_specs=vmem,
+        out_specs=[[vmem] * levels],
         scratch_shapes=[
             pltpu.VMEM((levels, parts) + diag_inverse.shape[1:], f32),
             pltpu.VMEM((levels, local, 2, order, order), bf),
@@ -446,6 +449,7 @@
         ),
     )(right_sides, diag_inverse, off_diagonal, target_snode, target_block, target_snode,
       target_block)
+    return jnp.stack(answers[0], axis=0)
 
 
 def program(right_sides, diag_inverse, off_diagonal, target_snode, target_block):

time: 83.3 us -> 82.5 us (level)
  local copies, waits for them, and re-layouts: 2.06 us -> 0 us
  other arithmetic: 0 us -> 2.04 us
    unnamed x1 -> x0, local copies, waits for them, and re-layouts: 2.06 us -> none
    another operation x0 -> x1, other arithmetic: none -> 2.04 us  [dense_on_device(): return jnp.stack(answers[0], axis=0)]
where the time goes in v7:
time: 82.5 us; the launch traced here: 82.4 us
  Pallas kernels  80.3 us (97%)
  other arithmetic  2.04 us (2%)
    pallas_call x1, Pallas kernels, dense_on_device(): pl.pallas_call(functools.partial(dense_kernel, n, parts), out_shape=[[jax...  80.3 us
    another operation x1, other arithmetic, dense_on_device(): return jnp.stack(answers[0], axis=0)  2.04 us

profile of v7, /device:TPU:0, one launch (start us, length us, event | category | flops | bytes accessed | tf_op | source)
XLA Modules:
  0.0 82.4 jit_solution(12172153334197173411)
XLA Ops:
  0.0 80.3 %shard_map.55 = (f32[2,256,128]{2,1,0:T(8,128)}, f32[2,256,128]{2,1,0:T(8,128)}, f32[2,256,128]{2,1,0:T(8,128)}) custom-call(f32[3,2,256,128]{3,2,1,0:T(8,128)} %rs_hbm.1, f32[3,2,64,256]{3,2,1,0:T(8,128)} %dg_ref.1, bf16[2,2,1024,256]{3,2,1,0:T(8,128)(2,1)} %od_hbm.1, s32[2,2,64]{2,1,0:T(2,128)} %snode_s.1, s32[2,2,64]{2,1,0:T(2,128)} %block_s.1, ...), custom_call_target="tpu_custom_call" | custom-call | tf_op jit(solution)/shard_map/pallas_call | solution.py:414
  80.3 2.0 %pad_maximum_fusion = f32[3,2,256,128]{3,2,1,0:T(8,128)} fusion(f32[1,2,256,128]{3,2,1,0:T(8,128)} %bitcast.5, f32[1,2,256,128]{3,2,1,0:T(8,128)} %bitcast.4, f32[1,2,256,128]{3,2,1,0:T(8,128)} %bitcast.3), kind=kLoop, calls=%fused_computation | loop fusion | flops 393216 | bytes 1572864 | tf_op jit(solution)/shard_map/stack | solution.py:452

commit v8 on v7

--- a/solution.py
+++ b/solution.py
@@ -258,6 +258,8 @@
     def z_copy(h, q, k):
         return remote(zs.at[h, q, k], rz.at[h, q, k], zsend.at[h, q, k], zrecv.at[h, q, k], peers[k])
 
+    last = [(cut - 1, away[-1]), (cut - 1, 0)]
+    released = [(q, k) for q in range(cut) for k in away + [0] if (q, k) not in last]
     first = start_gather(0)
     tables = []
     rows = lax.broadcasted_iota(jnp.int32, (n * local_rows, outgoing), 0)
@@ -306,17 +308,16 @@
 
         for q in range(cut):
             for k in away:
+                if h == 0 and (q, k) == (cut - 1, away[-1]):
+                    for early in released:
+                        x_copy(h, *early).wait_send()
+
+                    @pl.when(cc == 1)
+                    def _():
+                        pl.semaphore_signal(token, inc=1, device_id=twin, device_id_type=MESH)
+
                 zs[h, q, k] = paired(q, k).astype(jnp.bfloat16)
                 z_copy(h, q, k).start()
-        if h == 0:
-            for q in range(cut):
-                for k in range(line):
-                    x_copy(h, q, k).wait_send()
-
-            @pl.when(cc == 1)
-            def _():
-                pl.semaphore_signal(token, inc=1, device_id=twin, device_id_type=MESH)
-
         if h == 0:
             prepare(0)
         finish_gather(h + 1, *gather[h + 1])
@@ -387,7 +388,7 @@
     for h in range(levels - 1):
         for q in range(cut):
             for k in range(line):
-                if h > 0:
+                if h > 0 or (q, k) not in released:
                     x_copy(h, q, k).wait_send()
                 mate_hop(h, q, k, x).wait_send()
             for k in away:

time: 82.5 us -> 81.8 us (level)
  no operation moved by 1% of the time
where the time goes in v8:
time: 81.8 us; the launch traced here: 81.6 us
  Pallas kernels  79.6 us (97%)
  other arithmetic  2.04 us (2%)
    pallas_call x1, Pallas kernels, dense_on_device(): pl.pallas_call(functools.partial(dense_kernel, n, parts), out_shape=[[jax...  79.6 us
    another operation x1, other arithmetic, dense_on_device(): return jnp.stack(answers[0], axis=0)  2.04 us

profile of v8, /device:TPU:0, one launch (start us, length us, event | category | flops | bytes accessed | tf_op | source)
XLA Modules:
  0.0 81.6 jit_solution(14606415543068504905)
XLA Ops:
  0.0 79.6 %shard_map.55 = (f32[2,256,128]{2,1,0:T(8,128)}, f32[2,256,128]{2,1,0:T(8,128)}, f32[2,256,128]{2,1,0:T(8,128)}) custom-call(f32[3,2,256,128]{3,2,1,0:T(8,128)} %rs_hbm.1, f32[3,2,64,256]{3,2,1,0:T(8,128)} %dg_ref.1, bf16[2,2,1024,256]{3,2,1,0:T(8,128)(2,1)} %od_hbm.1, s32[2,2,64]{2,1,0:T(2,128)} %snode_s.1, s32[2,2,64]{2,1,0:T(2,128)} %block_s.1, ...), custom_call_target="tpu_custom_call" | custom-call | tf_op jit(solution)/shard_map/pallas_call | solution.py:415
  79.6 2.0 %pad_maximum_fusion = f32[3,2,256,128]{3,2,1,0:T(8,128)} fusion(f32[1,2,256,128]{3,2,1,0:T(8,128)} %bitcast.5, f32[1,2,256,128]{3,2,1,0:T(8,128)} %bitcast.4, f32[1,2,256,128]{3,2,1,0:T(8,128)} %bitcast.3), kind=kLoop, calls=%fused_computation | loop fusion | flops 393216 | bytes 1572864 | tf_op jit(solution)/shard_map/stack | solution.py:453
